TPU v7x, 128 devices: a whole 4x4x4 slice. The times are simulated.
128 devices in a mesh: bx: 16 (over z, x), bz: 8 (over y, core).
Axes of the slice: x: 4, y: 4, z: 4, core: 2. Of those that a mesh axis runs over, the one named last changes fastest.
Arguments:
- fields: bfloat16 [4, 64, 1024, 4096], P(None, 'bz', None, 'bx'), may hold values from -6 to 6
- breakpoints: int32 [8], replicated, may hold values from 0 to 255, as said below
- tf_color: float32 [8, 3], replicated, may hold values from 0.05 to 1
- tf_opacity: float32 [8], replicated, may hold values from 0.002 to 0.02
- depth_order: int32 [16, 8], replicated, may hold values from 0 to 7, each once within a row
- live_rows: int32 [16, 8, 2], P('bx', 'bz'), may hold values from 0 to 1024, as said below
Outputs:
- image: float32 [4, 1024, 4096], P(None, ('bx', 'bz'))
Inputs may be any that keep to these rules, and one draw needn't show every extreme that they name: `breakpoints`: strictly increasing, first 0 and last 255. `live_rows`: for every brick the first row is below 512 and the end row above it; some brick starts at row 0 and some ends at row 1024.
All inputs are finite; a program needn't handle non-finite values.
Results may differ from a plain program's by a relative error of at most 0.0003.
Values may be sent and summed in bfloat16 or wider, within the bound.
No kernel may reach another device: no remote copies, remote signals or barrier semaphores. Data moves between devices by JAX's collectives and lax.ppermute only.
A program may use at most 128 MiB of HBM per device.

v0:
```python
import jax
import jax.numpy as jnp
from jax import lax
from jax.sharding import PartitionSpec as P

NBP = 8


def from_behind(block, axis, distance):
    devices = range(lax.axis_size(axis))
    route = [(i - distance, i) for i in devices if i - distance in devices]
    return lax.ppermute(block, axis, route)


def classify(raw, breakpoints, tf_color, tf_opacity):
    level = 255.0 * jax.nn.sigmoid(raw[0])
    swirl = raw[1] * raw[1] + raw[2] * raw[2] + raw[3] * raw[3]
    marks = breakpoints.astype(jnp.float32)
    ramps = []
    for j in range(1, NBP):
        ramps.append(jnp.clip((level - marks[j - 1]) / (marks[j] - marks[j - 1]), 0.0, 1.0))

    def lookup(values):
        total = values[0] + jnp.zeros_like(level)
        for j in range(1, NBP):
            total = total + (values[j] - values[j - 1]) * ramps[j - 1]
        return total

    alpha = 1.0 - jnp.exp(-lookup(tf_opacity) * (0.25 + swirl))
    return jnp.stack(
        [
            alpha * lookup(tf_color[:, 0]),
            alpha * lookup(tf_color[:, 1]),
            alpha * lookup(tf_color[:, 2]),
            alpha,
        ]
    )


def composite(gathered, order_rows):
    depth_count = gathered.shape[2]
    slots = jnp.arange(depth_count, dtype=jnp.int32)
    result = jnp.zeros((4, gathered.shape[1], gathered.shape[3], gathered.shape[4]), jnp.float32)
    for k in range(depth_count):
        pick = (order_rows[:, k][:, None] == slots[None, :]).astype(jnp.float32)
        chosen = jnp.sum(gathered * pick[None, :, :, None, None], axis=2)
        result = result + (1.0 - result[3:4]) * chosen
    return result


def per_device(fields, breakpoints, tf_color, tf_opacity, depth_order, live_rows):
    width = fields.shape[3]
    slices = fields.shape[1]
    height = fields.shape[2]
    count_x = lax.axis_size("bx")
    count_z = lax.axis_size("bz")
    reach = 3 * (slices * count_z - 1) // 8 + 1
    rim = from_behind(fields[:, :, :, width - reach :], "bx", 1)
    edge = (lax.axis_index("bx") > 0).astype(jnp.float32)
    column_keep = jnp.concatenate(
        [jnp.zeros((reach,), jnp.float32) + edge, jnp.ones((width,), jnp.float32)]
    )
    zbase = lax.axis_index("bz") * slices

    def advance(k, acc):
        raw = jnp.concatenate(
            [
                lax.dynamic_index_in_dim(rim, k, 1, keepdims=False),
                lax.dynamic_index_in_dim(fields, k, 1, keepdims=False),
            ],
            axis=2,
        ).astype(jnp.float32)
        sample = classify(raw, breakpoints, tf_color, tf_opacity) * column_keep[None, None, :]
        zglobal = zbase + k
        whole = 3 * zglobal // 8
        frac = (3 * zglobal % 8).astype(jnp.float32) / 8.0
        near = lax.dynamic_slice_in_dim(sample, reach - whole, width, 2)
        far = lax.dynamic_slice_in_dim(sample, reach - whole - 1, width, 2)
        return acc + (1.0 - acc[3:4]) * ((1.0 - frac) * near + frac * far)

    partial_value = lax.fori_loop(0, slices, advance, jnp.zeros((4, height, width), jnp.float32))
    rows = jnp.arange(height, dtype=jnp.int32)
    keep = ((rows >= live_rows[0, 0, 0]) & (rows < live_rows[0, 0, 1])).astype(jnp.float32)
    partial_value = partial_value * keep[None, :, None]
    owned = height // (count_x * count_z)
    pieces = partial_value.reshape(4, count_x * count_z, owned, width)
    arrived = lax.all_to_all(pieces, ("bx", "bz"), split_axis=1, concat_axis=1, tiled=True).reshape(
        4, count_x, count_z, owned, width
    )
    merged = composite(arrived, depth_order)
    image = merged.transpose(0, 2, 1, 3).reshape(4, owned, count_x * width)
    return image


def solution(mesh):
    return jax.shard_map(
        per_device,
        mesh=mesh,
        in_specs=(P(None, "bz", None, "bx"), P(), P(), P(), P(), P("bx", "bz", None)),
        out_specs=P(None, ("bx", "bz"), None),
        check_vma=False,
    )
```

profile of v0, /device:TPU:1, one launch (start us, length us, event | category | flops | bytes accessed | tf_op | source)
XLA Modules:
  0.0 486.1 jit_solution(9143653285680278266)
XLA Ops:
  0.0 9.0 %slice.675 = bf16[4,8,1024,24]{3,2,1,0:T(8,128)(2,1)} slice(bf16[4,8,1024,256]{3,2,1,0:T(8,128)(2,1)} %param.8), slice={[0:4], [0:8], [0:1024], [232:256]} | slice | bytes 3145728 | tf_op jit(solution)/shard_map/slice | solution.py:58
  9.0 6.7 %copy.33 = bf16[4,8,1024,24]{2,3,1,0:T(8,128)(2,1)S(1)} copy(bf16[4,8,1024,24]{3,2,1,0:T(8,128)(2,1)} %slice.675) | data formatting | bytes 3145728
  15.8 5.2 %collective-permute-start = (bf16[4,8,1024,24]{2,3,1,0:T(8,128)(2,1)S(1)}, bf16[4,8,1024,24]{2,3,1,0:T(8,128)(2,1)}, u32[]{:S(2)}, u32[]{:S(2)}) collective-permute-start(bf16[4,8,1024,24]{2,3,1,0:T(8,128)(2,1)S(1)} %copy.33), channel_id=1, source_target_pairs={{0,8},{8,16},{16,24},{24,32},{32,40},{40,48},{48,56},{56,64},{64,7... | collective-permute-start | bytes 4718600 | tf_op jit(solution)/shard_map/ppermute | solution.py:12
  69.0 334.1 %while.19 = (s32[]{:T(128)}, f32[4,1024,256]{1,2,0:T(8,128)}, s32[]{:T(128)}, f32[8]{0:T(128)S(1)}, f32[]{:T(128)}, /*index=5*/bf16[4,8,1024,24]{2,3,1,0:T(8,128...) while((s32[]{:T(128)}, f32[4,1024,256]{1,2,0:T(8,128)}, ...), condition=%wide.region_1.2_spmd.clone, body=%wide.region_0.1_spmd.clone.sunk | while | flops 57778176 | bytes 85264680 | solution.py:81
  69.0 3.1 constant_dynamic-slice_fusion.2
  77.8 7.6 %add_multiply_fusion.6 = (f32[1,1024,280]{1,2,0:T(8,128)S(1)}, f32[1,1024,280]{1,2,0:T(8,128)S(1)}) fusion(f32[]{:T(128)} %get-tuple-element.1830, f32[]{:T(128)} %get-tuple-element.1829, f32[]{:T(128)} %get-tuple-element.1828, f32[]{:T(128)} %get-tuple-element.1827, f32[]{:T(128)} %get-tuple-element.1826, f32[]{:T(128)} %get-tuple-element.1825, ...), kind=kLoop, calls=%fused_computation.20.clone.1 | loop fusion | flops 18063360 | bytes 6881400 | tf_op jit(solution)/shard_map/while/body/eval_jaxpr/mul | solution.py:32
  85.4 6.7 %add_multiply_fusion.8 = f32[1,1024,280]{1,2,0:T(8,128)S(1)} fusion(f32[1,1024,280]{1,2,0:T(8,128)S(1)} %get-tuple-element.1686, f32[]{:T(128)} %get-tuple-element.1837, f32[]{:T(128)} %get-tuple-element.1836, f32[]{:T(128)} %get-tuple-element.1835, f32[]{:T(128)} %get-tuple-element.1834, f32[]{:T(128)} %get-tuple-element.1833, ...), kind=kLoop, calls=%fused_computation.19.clone.1 | loop fusion | flops 11468800 | bytes 3440728 | tf_op jit(solution)/shard_map/while/body/eval_jaxpr/mul | solution.py:33
  92.1 6.6 %add_multiply_fusion.7 = f32[1,1024,280]{1,2,0:T(8,128)S(1)} fusion(f32[1,1024,280]{1,2,0:T(8,128)S(1)} %get-tuple-element.1686, f32[]{:T(128)} %get-tuple-element.1844, f32[]{:T(128)} %get-tuple-element.1843, f32[]{:T(128)} %get-tuple-element.1842, f32[]{:T(128)} %get-tuple-element.1841, f32[]{:T(128)} %get-tuple-element.1840, ...), kind=kLoop, calls=%fused_computation.18.clone.1 | loop fusion | flops 11468800 | bytes 3440728 | tf_op jit(solution)/shard_map/while/body/eval_jaxpr/mul | solution.py:34
  104.0 3.8 multiply_add_fusion.7
  107.7 3.1 constant_dynamic-slice_fusion.2
  116.5 7.6 %add_multiply_fusion.6 = (f32[1,1024,280]{1,2,0:T(8,128)S(1)}, f32[1,1024,280]{1,2,0:T(8,128)S(1)}) fusion(f32[]{:T(128)} %get-tuple-element.1830, f32[]{:T(128)} %get-tuple-element.1829, f32[]{:T(128)} %get-tuple-element.1828, f32[]{:T(128)} %get-tuple-element.1827, f32[]{:T(128)} %get-tuple-element.1826, f32[]{:T(128)} %get-tuple-element.1825, ...), kind=kLoop, calls=%fused_computation.20.clone.1 | loop fusion | flops 18063360 | bytes 6881400 | tf_op jit(solution)/shard_map/while/body/eval_jaxpr/mul | solution.py:32
  124.2 6.7 %add_multiply_fusion.8 = f32[1,1024,280]{1,2,0:T(8,128)S(1)} fusion(f32[1,1024,280]{1,2,0:T(8,128)S(1)} %get-tuple-element.1686, f32[]{:T(128)} %get-tuple-element.1837, f32[]{:T(128)} %get-tuple-element.1836, f32[]{:T(128)} %get-tuple-element.1835, f32[]{:T(128)} %get-tuple-element.1834, f32[]{:T(128)} %get-tuple-element.1833, ...), kind=kLoop, calls=%fused_computation.19.clone.1 | loop fusion | flops 11468800 | bytes 3440728 | tf_op jit(solution)/shard_map/while/body/eval_jaxpr/mul | solution.py:33
  130.8 6.6 %add_multiply_fusion.7 = f32[1,1024,280]{1,2,0:T(8,128)S(1)} fusion(f32[1,1024,280]{1,2,0:T(8,128)S(1)} %get-tuple-element.1686, f32[]{:T(128)} %get-tuple-element.1844, f32[]{:T(128)} %get-tuple-element.1843, f32[]{:T(128)} %get-tuple-element.1842, f32[]{:T(128)} %get-tuple-element.1841, f32[]{:T(128)} %get-tuple-element.1840, ...), kind=kLoop, calls=%fused_computation.18.clone.1 | loop fusion | flops 11468800 | bytes 3440728 | tf_op jit(solution)/shard_map/while/body/eval_jaxpr/mul | solution.py:34
  144.0 5.9 %multiply_add_fusion.7 = f32[4,1024,256]{1,2,0:T(8,128)} fusion(f32[4,1024,280]{1,2,0:T(8,128)S(1)} %copy-done, s32[]{:T(128)S(6)} %select_n.93, s32[]{:T(128)S(6)} %select_n.94, f32[]{:T(128)S(6)} %div.504, f32[]{:T(128)S(6)} %sub.1086, f32[1024,256]{0,1:T(8,128)S(1)} %fusion.57, f32[4,1024,256]{1,2,0:T(8,128)} %get-tuple-element.1747, pred[]{:T(512)S(6)} %compare.21), kind=kLoop, calls=%fused_computation.1.clone.1 | loop fusion | flops 6291456 | bytes 17825808 | tf_op jit(solution)/shard_map/while/body/eval_jaxpr/add | solution.py:79
  149.9 3.1 constant_dynamic-slice_fusion.2
  158.7 7.6 %add_multiply_fusion.6 = (f32[1,1024,280]{1,2,0:T(8,128)S(1)}, f32[1,1024,280]{1,2,0:T(8,128)S(1)}) fusion(f32[]{:T(128)} %get-tuple-element.1830, f32[]{:T(128)} %get-tuple-element.1829, f32[]{:T(128)} %get-tuple-element.1828, f32[]{:T(128)} %get-tuple-element.1827, f32[]{:T(128)} %get-tuple-element.1826, f32[]{:T(128)} %get-tuple-element.1825, ...), kind=kLoop, calls=%fused_computation.20.clone.1 | loop fusion | flops 18063360 | bytes 6881400 | tf_op jit(solution)/shard_map/while/body/eval_jaxpr/mul | solution.py:32
  166.3 6.7 %add_multiply_fusion.8 = f32[1,1024,280]{1,2,0:T(8,128)S(1)} fusion(f32[1,1024,280]{1,2,0:T(8,128)S(1)} %get-tuple-element.1686, f32[]{:T(128)} %get-tuple-element.1837, f32[]{:T(128)} %get-tuple-element.1836, f32[]{:T(128)} %get-tuple-element.1835, f32[]{:T(128)} %get-tuple-element.1834, f32[]{:T(128)} %get-tuple-element.1833, ...), kind=kLoop, calls=%fused_computation.19.clone.1 | loop fusion | flops 11468800 | bytes 3440728 | tf_op jit(solution)/shard_map/while/body/eval_jaxpr/mul | solution.py:33
  173.0 6.6 %add_multiply_fusion.7 = f32[1,1024,280]{1,2,0:T(8,128)S(1)} fusion(f32[1,1024,280]{1,2,0:T(8,128)S(1)} %get-tuple-element.1686, f32[]{:T(128)} %get-tuple-element.1844, f32[]{:T(128)} %get-tuple-element.1843, f32[]{:T(128)} %get-tuple-element.1842, f32[]{:T(128)} %get-tuple-element.1841, f32[]{:T(128)} %get-tuple-element.1840, ...), kind=kLoop, calls=%fused_computation.18.clone.1 | loop fusion | flops 11468800 | bytes 3440728 | tf_op jit(solution)/shard_map/while/body/eval_jaxpr/mul | solution.py:34
  186.2 5.9 %multiply_add_fusion.7 = f32[4,1024,256]{1,2,0:T(8,128)} fusion(f32[4,1024,280]{1,2,0:T(8,128)S(1)} %copy-done, s32[]{:T(128)S(6)} %select_n.93, s32[]{:T(128)S(6)} %select_n.94, f32[]{:T(128)S(6)} %div.504, f32[]{:T(128)S(6)} %sub.1086, f32[1024,256]{0,1:T(8,128)S(1)} %fusion.57, f32[4,1024,256]{1,2,0:T(8,128)} %get-tuple-element.1747, pred[]{:T(512)S(6)} %compare.21), kind=kLoop, calls=%fused_computation.1.clone.1 | loop fusion | flops 6291456 | bytes 17825808 | tf_op jit(solution)/shard_map/while/body/eval_jaxpr/add | solution.py:79
  192.1 3.1 constant_dynamic-slice_fusion.2
  200.9 7.6 %add_multiply_fusion.6 = (f32[1,1024,280]{1,2,0:T(8,128)S(1)}, f32[1,1024,280]{1,2,0:T(8,128)S(1)}) fusion(f32[]{:T(128)} %get-tuple-element.1830, f32[]{:T(128)} %get-tuple-element.1829, f32[]{:T(128)} %get-tuple-element.1828, f32[]{:T(128)} %get-tuple-element.1827, f32[]{:T(128)} %get-tuple-element.1826, f32[]{:T(128)} %get-tuple-element.1825, ...), kind=kLoop, calls=%fused_computation.20.clone.1 | loop fusion | flops 18063360 | bytes 6881400 | tf_op jit(solution)/shard_map/while/body/eval_jaxpr/mul | solution.py:32
  208.5 6.7 %add_multiply_fusion.8 = f32[1,1024,280]{1,2,0:T(8,128)S(1)} fusion(f32[1,1024,280]{1,2,0:T(8,128)S(1)} %get-tuple-element.1686, f32[]{:T(128)} %get-tuple-element.1837, f32[]{:T(128)} %get-tuple-element.1836, f32[]{:T(128)} %get-tuple-element.1835, f32[]{:T(128)} %get-tuple-element.1834, f32[]{:T(128)} %get-tuple-element.1833, ...), kind=kLoop, calls=%fused_computation.19.clone.1 | loop fusion | flops 11468800 | bytes 3440728 | tf_op jit(solution)/shard_map/while/body/eval_jaxpr/mul | solution.py:33
  215.2 6.6 %add_multiply_fusion.7 = f32[1,1024,280]{1,2,0:T(8,128)S(1)} fusion(f32[1,1024,280]{1,2,0:T(8,128)S(1)} %get-tuple-element.1686, f32[]{:T(128)} %get-tuple-element.1844, f32[]{:T(128)} %get-tuple-element.1843, f32[]{:T(128)} %get-tuple-element.1842, f32[]{:T(128)} %get-tuple-element.1841, f32[]{:T(128)} %get-tuple-element.1840, ...), kind=kLoop, calls=%fused_computation.18.clone.1 | loop fusion | flops 11468800 | bytes 3440728 | tf_op jit(solution)/shard_map/while/body/eval_jaxpr/mul | solution.py:34
  228.4 5.9 %multiply_add_fusion.7 = f32[4,1024,256]{1,2,0:T(8,128)} fusion(f32[4,1024,280]{1,2,0:T(8,128)S(1)} %copy-done, s32[]{:T(128)S(6)} %select_n.93, s32[]{:T(128)S(6)} %select_n.94, f32[]{:T(128)S(6)} %div.504, f32[]{:T(128)S(6)} %sub.1086, f32[1024,256]{0,1:T(8,128)S(1)} %fusion.57, f32[4,1024,256]{1,2,0:T(8,128)} %get-tuple-element.1747, pred[]{:T(512)S(6)} %compare.21), kind=kLoop, calls=%fused_computation.1.clone.1 | loop fusion | flops 6291456 | bytes 17825808 | tf_op jit(solution)/shard_map/while/body/eval_jaxpr/add | solution.py:79
  234.3 3.1 constant_dynamic-slice_fusion.2
  243.1 7.6 %add_multiply_fusion.6 = (f32[1,1024,280]{1,2,0:T(8,128)S(1)}, f32[1,1024,280]{1,2,0:T(8,128)S(1)}) fusion(f32[]{:T(128)} %get-tuple-element.1830, f32[]{:T(128)} %get-tuple-element.1829, f32[]{:T(128)} %get-tuple-element.1828, f32[]{:T(128)} %get-tuple-element.1827, f32[]{:T(128)} %get-tuple-element.1826, f32[]{:T(128)} %get-tuple-element.1825, ...), kind=kLoop, calls=%fused_computation.20.clone.1 | loop fusion | flops 18063360 | bytes 6881400 | tf_op jit(solution)/shard_map/while/body/eval_jaxpr/mul | solution.py:32
  250.7 6.7 %add_multiply_fusion.8 = f32[1,1024,280]{1,2,0:T(8,128)S(1)} fusion(f32[1,1024,280]{1,2,0:T(8,128)S(1)} %get-tuple-element.1686, f32[]{:T(128)} %get-tuple-element.1837, f32[]{:T(128)} %get-tuple-element.1836, f32[]{:T(128)} %get-tuple-element.1835, f32[]{:T(128)} %get-tuple-element.1834, f32[]{:T(128)} %get-tuple-element.1833, ...), kind=kLoop, calls=%fused_computation.19.clone.1 | loop fusion | flops 11468800 | bytes 3440728 | tf_op jit(solution)/shard_map/while/body/eval_jaxpr/mul | solution.py:33
  257.4 6.6 %add_multiply_fusion.7 = f32[1,1024,280]{1,2,0:T(8,128)S(1)} fusion(f32[1,1024,280]{1,2,0:T(8,128)S(1)} %get-tuple-element.1686, f32[]{:T(128)} %get-tuple-element.1844, f32[]{:T(128)} %get-tuple-element.1843, f32[]{:T(128)} %get-tuple-element.1842, f32[]{:T(128)} %get-tuple-element.1841, f32[]{:T(128)} %get-tuple-element.1840, ...), kind=kLoop, calls=%fused_computation.18.clone.1 | loop fusion | flops 11468800 | bytes 3440728 | tf_op jit(solution)/shard_map/while/body/eval_jaxpr/mul | solution.py:34
  270.6 5.9 %multiply_add_fusion.7 = f32[4,1024,256]{1,2,0:T(8,128)} fusion(f32[4,1024,280]{1,2,0:T(8,128)S(1)} %copy-done, s32[]{:T(128)S(6)} %select_n.93, s32[]{:T(128)S(6)} %select_n.94, f32[]{:T(128)S(6)} %div.504, f32[]{:T(128)S(6)} %sub.1086, f32[1024,256]{0,1:T(8,128)S(1)} %fusion.57, f32[4,1024,256]{1,2,0:T(8,128)} %get-tuple-element.1747, pred[]{:T(512)S(6)} %compare.21), kind=kLoop, calls=%fused_computation.1.clone.1 | loop fusion | flops 6291456 | bytes 17825808 | tf_op jit(solution)/shard_map/while/body/eval_jaxpr/add | solution.py:79
  276.5 3.1 constant_dynamic-slice_fusion.2
  285.3 7.6 %add_multiply_fusion.6 = (f32[1,1024,280]{1,2,0:T(8,128)S(1)}, f32[1,1024,280]{1,2,0:T(8,128)S(1)}) fusion(f32[]{:T(128)} %get-tuple-element.1830, f32[]{:T(128)} %get-tuple-element.1829, f32[]{:T(128)} %get-tuple-element.1828, f32[]{:T(128)} %get-tuple-element.1827, f32[]{:T(128)} %get-tuple-element.1826, f32[]{:T(128)} %get-tuple-element.1825, ...), kind=kLoop, calls=%fused_computation.20.clone.1 | loop fusion | flops 18063360 | bytes 6881400 | tf_op jit(solution)/shard_map/while/body/eval_jaxpr/mul | solution.py:32
  292.9 6.7 %add_multiply_fusion.8 = f32[1,1024,280]{1,2,0:T(8,128)S(1)} fusion(f32[1,1024,280]{1,2,0:T(8,128)S(1)} %get-tuple-element.1686, f32[]{:T(128)} %get-tuple-element.1837, f32[]{:T(128)} %get-tuple-element.1836, f32[]{:T(128)} %get-tuple-element.1835, f32[]{:T(128)} %get-tuple-element.1834, f32[]{:T(128)} %get-tuple-element.1833, ...), kind=kLoop, calls=%fused_computation.19.clone.1 | loop fusion | flops 11468800 | bytes 3440728 | tf_op jit(solution)/shard_map/while/body/eval_jaxpr/mul | solution.py:33
  299.6 6.6 %add_multiply_fusion.7 = f32[1,1024,280]{1,2,0:T(8,128)S(1)} fusion(f32[1,1024,280]{1,2,0:T(8,128)S(1)} %get-tuple-element.1686, f32[]{:T(128)} %get-tuple-element.1844, f32[]{:T(128)} %get-tuple-element.1843, f32[]{:T(128)} %get-tuple-element.1842, f32[]{:T(128)} %get-tuple-element.1841, f32[]{:T(128)} %get-tuple-element.1840, ...), kind=kLoop, calls=%fused_computation.18.clone.1 | loop fusion | flops 11468800 | bytes 3440728 | tf_op jit(solution)/shard_map/while/body/eval_jaxpr/mul | solution.py:34
  312.8 5.9 %multiply_add_fusion.7 = f32[4,1024,256]{1,2,0:T(8,128)} fusion(f32[4,1024,280]{1,2,0:T(8,128)S(1)} %copy-done, s32[]{:T(128)S(6)} %select_n.93, s32[]{:T(128)S(6)} %select_n.94, f32[]{:T(128)S(6)} %div.504, f32[]{:T(128)S(6)} %sub.1086, f32[1024,256]{0,1:T(8,128)S(1)} %fusion.57, f32[4,1024,256]{1,2,0:T(8,128)} %get-tuple-element.1747, pred[]{:T(512)S(6)} %compare.21), kind=kLoop, calls=%fused_computation.1.clone.1 | loop fusion | flops 6291456 | bytes 17825808 | tf_op jit(solution)/shard_map/while/body/eval_jaxpr/add | solution.py:79
  318.7 3.1 constant_dynamic-slice_fusion.2
  327.5 7.6 %add_multiply_fusion.6 = (f32[1,1024,280]{1,2,0:T(8,128)S(1)}, f32[1,1024,280]{1,2,0:T(8,128)S(1)}) fusion(f32[]{:T(128)} %get-tuple-element.1830, f32[]{:T(128)} %get-tuple-element.1829, f32[]{:T(128)} %get-tuple-element.1828, f32[]{:T(128)} %get-tuple-element.1827, f32[]{:T(128)} %get-tuple-element.1826, f32[]{:T(128)} %get-tuple-element.1825, ...), kind=kLoop, calls=%fused_computation.20.clone.1 | loop fusion | flops 18063360 | bytes 6881400 | tf_op jit(solution)/shard_map/while/body/eval_jaxpr/mul | solution.py:32
  335.1 6.7 %add_multiply_fusion.8 = f32[1,1024,280]{1,2,0:T(8,128)S(1)} fusion(f32[1,1024,280]{1,2,0:T(8,128)S(1)} %get-tuple-element.1686, f32[]{:T(128)} %get-tuple-element.1837, f32[]{:T(128)} %get-tuple-element.1836, f32[]{:T(128)} %get-tuple-element.1835, f32[]{:T(128)} %get-tuple-element.1834, f32[]{:T(128)} %get-tuple-element.1833, ...), kind=kLoop, calls=%fused_computation.19.clone.1 | loop fusion | flops 11468800 | bytes 3440728 | tf_op jit(solution)/shard_map/while/body/eval_jaxpr/mul | solution.py:33
  341.8 6.6 %add_multiply_fusion.7 = f32[1,1024,280]{1,2,0:T(8,128)S(1)} fusion(f32[1,1024,280]{1,2,0:T(8,128)S(1)} %get-tuple-element.1686, f32[]{:T(128)} %get-tuple-element.1844, f32[]{:T(128)} %get-tuple-element.1843, f32[]{:T(128)} %get-tuple-element.1842, f32[]{:T(128)} %get-tuple-element.1841, f32[]{:T(128)} %get-tuple-element.1840, ...), kind=kLoop, calls=%fused_computation.18.clone.1 | loop fusion | flops 11468800 | bytes 3440728 | tf_op jit(solution)/shard_map/while/body/eval_jaxpr/mul | solution.py:34
  355.0 5.9 %multiply_add_fusion.7 = f32[4,1024,256]{1,2,0:T(8,128)} fusion(f32[4,1024,280]{1,2,0:T(8,128)S(1)} %copy-done, s32[]{:T(128)S(6)} %select_n.93, s32[]{:T(128)S(6)} %select_n.94, f32[]{:T(128)S(6)} %div.504, f32[]{:T(128)S(6)} %sub.1086, f32[1024,256]{0,1:T(8,128)S(1)} %fusion.57, f32[4,1024,256]{1,2,0:T(8,128)} %get-tuple-element.1747, pred[]{:T(512)S(6)} %compare.21), kind=kLoop, calls=%fused_computation.1.clone.1 | loop fusion | flops 6291456 | bytes 17825808 | tf_op jit(solution)/shard_map/while/body/eval_jaxpr/add | solution.py:79
  360.9 3.1 constant_dynamic-slice_fusion.2
  369.7 7.6 %add_multiply_fusion.6 = (f32[1,1024,280]{1,2,0:T(8,128)S(1)}, f32[1,1024,280]{1,2,0:T(8,128)S(1)}) fusion(f32[]{:T(128)} %get-tuple-element.1830, f32[]{:T(128)} %get-tuple-element.1829, f32[]{:T(128)} %get-tuple-element.1828, f32[]{:T(128)} %get-tuple-element.1827, f32[]{:T(128)} %get-tuple-element.1826, f32[]{:T(128)} %get-tuple-element.1825, ...), kind=kLoop, calls=%fused_computation.20.clone.1 | loop fusion | flops 18063360 | bytes 6881400 | tf_op jit(solution)/shard_map/while/body/eval_jaxpr/mul | solution.py:32
  377.3 6.7 %add_multiply_fusion.8 = f32[1,1024,280]{1,2,0:T(8,128)S(1)} fusion(f32[1,1024,280]{1,2,0:T(8,128)S(1)} %get-tuple-element.1686, f32[]{:T(128)} %get-tuple-element.1837, f32[]{:T(128)} %get-tuple-element.1836, f32[]{:T(128)} %get-tuple-element.1835, f32[]{:T(128)} %get-tuple-element.1834, f32[]{:T(128)} %get-tuple-element.1833, ...), kind=kLoop, calls=%fused_computation.19.clone.1 | loop fusion | flops 11468800 | bytes 3440728 | tf_op jit(solution)/shard_map/while/body/eval_jaxpr/mul | solution.py:33
  384.0 6.6 %add_multiply_fusion.7 = f32[1,1024,280]{1,2,0:T(8,128)S(1)} fusion(f32[1,1024,280]{1,2,0:T(8,128)S(1)} %get-tuple-element.1686, f32[]{:T(128)} %get-tuple-element.1844, f32[]{:T(128)} %get-tuple-element.1843, f32[]{:T(128)} %get-tuple-element.1842, f32[]{:T(128)} %get-tuple-element.1841, f32[]{:T(128)} %get-tuple-element.1840, ...), kind=kLoop, calls=%fused_computation.18.clone.1 | loop fusion | flops 11468800 | bytes 3440728 | tf_op jit(solution)/shard_map/while/body/eval_jaxpr/mul | solution.py:34
  397.2 5.9 %multiply_add_fusion.7 = f32[4,1024,256]{1,2,0:T(8,128)} fusion(f32[4,1024,280]{1,2,0:T(8,128)S(1)} %copy-done, s32[]{:T(128)S(6)} %select_n.93, s32[]{:T(128)S(6)} %select_n.94, f32[]{:T(128)S(6)} %div.504, f32[]{:T(128)S(6)} %sub.1086, f32[1024,256]{0,1:T(8,128)S(1)} %fusion.57, f32[4,1024,256]{1,2,0:T(8,128)} %get-tuple-element.1747, pred[]{:T(512)S(6)} %compare.21), kind=kLoop, calls=%fused_computation.1.clone.1 | loop fusion | flops 6291456 | bytes 17825808 | tf_op jit(solution)/shard_map/while/body/eval_jaxpr/add | solution.py:79
  403.1 5.4 %copy.28 = f32[4,1024,256]{2,1,0:T(8,128)} copy(f32[4,1024,256]{1,2,0:T(8,128)} %get-tuple-element.823) | data formatting | bytes 8388608 | tf_op jit(solution)/shard_map/while | solution.py:81
  413.6 10.1 %all-to-all-start = ((f32[4,128,8,256]{3,2,0,1:T(8,128)}), f32[4,128,8,256]{3,2,0,1:T(8,128)}, u32[]{:S(2)}, u32[]{:S(2)}) async-start(f32[4,128,8,256]{3,2,0,1:T(8,128)} %copy.29), calls=%async_computation | async-start | bytes 8388608 | tf_op jit(solution)/shard_map/all_to_all | solution.py:87
  424.1 52.5 %all-to-all-done = f32[4,128,8,256]{3,2,0,1:T(8,128)} async-done(((f32[4,128,8,256]{3,2,0,1:T(8,128)}), f32[4,128,8,256]{3,2,0,1:T(8,128)}, u32[]{:S(2)}, u32[]{:S(2)}) %all-to-all-start) | async-done | bytes 4194336 | tf_op jit(solution)/shard_map/all_to_all | solution.py:87
  476.6 7.3 %multiply_reduce_fusion.7 = (f32[4,16,8,256]{3,2,0,1:T(8,128)S(1)}, f32[4,16,8,256]{3,2,0,1:T(8,128)S(1)}, f32[4,16,8,256]{3,2,0,1:T(8,128)S(1)}, f32[4,16,8,256...) fusion(f32[16,8]{1,0:T(8,128)S(1)} %get-tuple-element.1393, ...), kind=kLoop, calls=%fused_computation.39 | loop fusion | flops 15728640 | bytes 8392704 | tf_op jit(solution)/shard_map/reduce_sum | solution.py:46
  (122 shorter events, 108.8 us)
Async XLA Ops:
  9.0 11.9 %copy-start.1 = (f32[8,3]{0,1:T(4,128)S(1)}, f32[8,3]{0,1:T(4,128)}, u32[]{:S(2)}) copy-start(f32[8,3]{0,1:T(4,128)} %param.10) | copy-start | bytes 292
  9.0 34.6 %copy-start.5 = (s32[8]{0:T(128)S(1)}, s32[8]{0:T(128)}, u32[]{:S(2)}) copy-start(s32[8]{0:T(128)} %param.9) | copy-start | bytes 100
  9.0 43.8 %copy-start.2 = (f32[8]{0:T(128)S(1)}, f32[8]{0:T(128)}, u32[]{:S(2)}) copy-start(f32[8]{0:T(128)} %param.11) | copy-start | bytes 100
  9.0 58.1 %copy-start.4 = (s32[1,1,2]{2,1,0:T(1,128)S(1)}, s32[1,1,2]{2,1,0:T(1,128)}, u32[]{:S(2)}) copy-start(s32[1,1,2]{2,1,0:T(1,128)} %param.13) | copy-start | bytes 28
  15.8 53.2 %collective-permute-start = (bf16[4,8,1024,24]{2,3,1,0:T(8,128)(2,1)S(1)}, bf16[4,8,1024,24]{2,3,1,0:T(8,128)(2,1)}, u32[]{:S(2)}, u32[]{:S(2)}) collective-permute-start(bf16[4,8,1024,24]{2,3,1,0:T(8,128)(2,1)S(1)} %copy.33), channel_id=1, source_target_pairs={{0,8},{8,16},{16,24},{24,32},{32,40},{40,48},{48,56},{56,64},{64,7... | collective-permute-start | bytes 4718600 | tf_op jit(solution)/shard_map/ppermute | solution.py:12
  101.7 2.3 copy-start
  140.4 3.6 copy-start
  182.6 3.6 copy-start
  224.8 3.6 copy-start
  267.0 3.6 copy-start
  309.2 3.6 copy-start
  351.4 3.6 copy-start
  393.6 3.6 copy-start
  413.6 10.1 %copy-start.3 = (s32[16,8]{0,1:T(8,128)S(1)}, s32[16,8]{0,1:T(8,128)}, u32[]{:S(2)}) copy-start(s32[16,8]{0,1:T(8,128)} %param.12) | copy-start | bytes 1540
  413.6 62.9 %all-to-all-start = ((f32[4,128,8,256]{3,2,0,1:T(8,128)}), f32[4,128,8,256]{3,2,0,1:T(8,128)}, u32[]{:S(2)}, u32[]{:S(2)}) async-start(f32[4,128,8,256]{3,2,0,1:T(8,128)} %copy.29), calls=%async_computation | async-start | bytes 8388608 | tf_op jit(solution)/shard_map/all_to_all | solution.py:87
where the time goes:
time: 490 us; the launch traced here: 486 us
  other arithmetic  273 us (56%)
  local copies, waits for them, and re-layouts  101 us (21%)
  waiting for transfers between devices  52.5 us (11%)
  between operations  43.6 us (9%)
  starting transfers between devices  15.3 us (3%)
    mul x8, other arithmetic, classify(): alpha * lookup(tf_color[:, 0])  60.8 us
    mul x8, other arithmetic, classify(): alpha * lookup(tf_color[:, 1])  53.4 us
    mul x8, other arithmetic, classify(): alpha * lookup(tf_color[:, 2])  52.8 us
    all_to_all x1, waiting for transfers between devices, per_device(): lax.all_to_all(pieces, ('bx', 'bz'), split_axis=1, concat_axis=1, tiled=T...  52.5 us
    dynamic_slice x16, local copies, waits for them, and re-layouts, advance(): lax.dynamic_index_in_dim(fields, k, 1, keepdims=False)  48.5 us
    add x8, other arithmetic, advance(): return acc + (1.0 - acc[3:4]) * ((1.0 - frac) * near + frac * far)  45.3 us
    mul x8, other arithmetic, advance(): classify(raw, breakpoints, tf_color, tf_opacity)  24 us
    while x8, other arithmetic  19.9 us
  transfers between devices with their start and end apart: 2, of which 1 were waited for; matrix products, arithmetic and copies ran while one was open for 1% of the time, Pallas kernels for 0%

commit v1 on v0

v1 whole, which is shorter than its diff:
```python
import functools

import jax
import jax.numpy as jnp
from jax import lax
from jax.experimental import pallas as pl
from jax.experimental.pallas import tpu as pltpu
from jax.sharding import PartitionSpec as P

NBP = 8
LANES = 128
TILE = 8
BLOCK = 128
HALF = BLOCK // 2
CODE = 65534.0
LOG2E = 1.4426950408889634
LOOKUP = "gather"


def tables(bp_ref, color_ref, opacity_ref):
    marks = [bp_ref[j].astype(jnp.float32) * (1.0 / 127.5) - 1.0 for j in range(NBP)]
    values = [[color_ref[j, c] for j in range(NBP)] for c in range(3)]
    values.append([opacity_ref[j] for j in range(NBP)])
    row = lax.broadcasted_iota(jnp.int32, (TILE, LANES), 0)

    def by_segment(scalars):
        table = jnp.full((TILE, LANES), scalars[0], jnp.float32)
        for j in range(1, NBP - 1):
            table = jnp.where(row >= j, scalars[j], table)
        return table

    low = by_segment(marks[: NBP - 1])
    width = by_segment(marks[1:]) - low
    pairs = []
    for c, value in enumerate(values):
        start = by_segment(value[: NBP - 1])
        slope = (by_segment(value[1:]) - start) / width
        offset = start - slope * low
        if c == 3:
            slope, offset = -LOG2E * slope, -LOG2E * offset
        pairs.append((offset, slope))
    return marks, pairs


def classify(raw, marks, pairs):
    h = jnp.tanh(raw[0] * 0.5)
    swirl = raw[1] * raw[1] + raw[2] * raw[2] + (raw[3] * raw[3] + 0.25)
    index = jnp.zeros(h.shape, jnp.int32)
    for j in range(1, NBP - 1):
        index = jnp.where(h >= marks[j], j, index)
    looked = []
    for offset, slope in pairs:
        parts = []
        for r in range(0, h.shape[0], TILE):
            own = index[r : r + TILE]
            parts.append(
                jnp.take_along_axis(offset, own, axis=0, mode="promise_in_bounds")
                + jnp.take_along_axis(slope, own, axis=0, mode="promise_in_bounds") * h[r : r + TILE]
            )
        looked.append(parts[0] if len(parts) == 1 else jnp.concatenate(parts, axis=0))
    return looked[:3], jnp.exp2(looked[3] * swirl)


def steps(slices):
    return [(3 * k // 8, (3 * k % 8) / 8.0) for k in range(slices)]


def encode(value):
    return (jnp.sqrt(value) * CODE + 0.5).astype(jnp.int32) - 32767


def boundary(halo_ref, own_ref, keep, marks, pairs, slices, edge_ref):
    lane = lax.broadcasted_iota(jnp.int32, (HALF, LANES), 1)
    slot = lax.rem(lane, 8)
    slab = lax.rem(lax.div(lane, 8), 8)
    raw = []
    for f in range(4):
        raw.append(jnp.where(slot < 3, halo_ref[f].astype(jnp.float32), own_ref[f].astype(jnp.float32)))
    color, through = classify(raw, marks, pairs)
    if keep is not None:
        through = jnp.where((slot < 3) & (keep == 0), 1.0, through)
    alpha = 1.0 - through
    samples = [alpha * c for c in color] + [through]
    whole = lax.div(3 * slab, 8)
    frac = lax.rem(3 * slab, 8).astype(jnp.float32) * 0.125
    sheared = [jnp.zeros((HALF, LANES), jnp.float32)] * 4
    for s in range(steps(slices)[-1][0] + 2):
        weight = jnp.where(whole == s, 1.0 - frac, 0.0) + jnp.where(whole + 1 == s, frac, 0.0)
        for c in range(4):
            moved = samples[c] if s == 0 else pltpu.roll(samples[c], s, 1)
            sheared[c] = sheared[c] + weight * moved
    product = sheared[3]
    for s in (1, 2, 4):
        product = product * jnp.where(slab >= s, pltpu.roll(product, 8 * s, 1), 1.0)
    before = jnp.where(slab >= 1, pltpu.roll(product, 8, 1), 1.0)
    for c in range(3):
        total = before * sheared[c]
        for s in (1, 2, 4):
            total = total + jnp.where(slab >= s, pltpu.roll(total, 8 * s, 1), 0.0)
        edge_ref[c] = total
    edge_ref[3] = 1.0 - product


def brick_kernel(slices, right, bp_ref, color_ref, opacity_ref, place_ref, fields_ref, halo_ref, own_ref, out_ref, edge_ref):
    marks, pairs = tables(bp_ref, color_ref, opacity_ref)
    boundary(halo_ref, own_ref, None if right else place_ref[0], marks, pairs, slices, edge_ref)
    plan = steps(slices)
    first = pl.program_id(0) * BLOCK
    rows = 2 * TILE

    def group(j, carry):
        base = pl.multiple_of(j * rows, rows)
        acc = [jnp.zeros((rows, LANES), jnp.float32) for _ in range(3)]
        far = [jnp.zeros((rows, LANES), jnp.float32) for _ in range(3)]
        through = jnp.ones((rows, LANES), jnp.float32)
        at = 0
        for k in range(slices):
            whole, frac = plan[k]
            if whole != at:
                acc = [pltpu.roll(a, LANES - (whole - at), 1) for a in acc]
                far = [pltpu.roll(a, LANES - (whole - at), 1) for a in far]
                through = pltpu.roll(through, LANES - (whole - at), 1)
                at = whole
            raw = [fields_ref[f, k, pl.ds(base, rows), :].astype(jnp.float32) for f in range(4)]
            color, clear = classify(raw, marks, pairs)
            alpha = 1.0 - clear
            near_t = through * (1.0 - frac) if frac else through
            near_w = near_t * alpha
            acc = [a + near_w * c for a, c in zip(acc, color)]
            if frac:
                far_t = through * frac
                far_w = pltpu.roll(far_t, LANES - 1, 1) * alpha
                far = [a + far_w * c for a, c in zip(far, color)]
                through = near_t * clear + far_t * pltpu.roll(clear, 1, 1)
            else:
                through = near_t * clear
        back = at
        done = [pltpu.roll(a + pltpu.roll(b, 1, 1), back, 1) for a, b in zip(acc, far)]
        done.append(1.0 - pltpu.roll(through, back, 1))
        lane = lax.broadcasted_iota(jnp.int32, (TILE, LANES), 1)
        for r in range(2):
            tile = 2 * j + r
            side = lax.div(tile, HALF // TILE)
            spot = pl.multiple_of((tile - side * (HALF // TILE)) * TILE, TILE)
            turn = lax.rem(LANES + LANES - (64 * side + 8 * (slices - 1) + 3), LANES)
            row = lax.broadcasted_iota(jnp.int32, (TILE, LANES), 0) + (first + tile * TILE)
            low, high = place_ref[1], place_ref[2]
            if right:
                inside = lane < place_ref[5]
                low = jnp.where(inside, low, place_ref[3])
                high = jnp.where(inside, high, place_ref[4])
            live = (row >= low) & (row < high)
            codes = []
            for c in range(4):
                value = done[c][r * TILE : (r + 1) * TILE]
                edge = pltpu.roll(edge_ref[c, pl.ds(spot, TILE), :], turn, 1)
                value = jnp.where(lane < 3, edge, value)
                value = jnp.where(live, jnp.maximum(value, 0.0), 0.0)
                codes.append(encode(value))
            out_ref[tile] = jnp.concatenate(codes, axis=0).astype(jnp.int16)
        return carry

    lax.fori_loop(0, BLOCK // rows, group, 0)


def brick_half(right, breakpoints, tf_color, tf_opacity, place, fields, halo, own):
    slices, height = fields.shape[1], fields.shape[2]
    half = 1 if right else 0
    smem = pl.BlockSpec(memory_space=pltpu.SMEM)
    compact = pl.BlockSpec((4, HALF, LANES), lambda i: (0, i, 0))
    return pl.pallas_call(
        functools.partial(brick_kernel, slices, right),
        grid=(height // BLOCK,),
        in_specs=[smem, smem, smem, smem, pl.BlockSpec((4, slices, BLOCK, LANES), lambda i: (0, 0, i, half)), compact, compact],
        out_specs=pl.BlockSpec((BLOCK // TILE, 4 * TILE, LANES), lambda i: (i, 0, 0)),
        out_shape=jax.ShapeDtypeStruct((height // TILE, 4 * TILE, LANES), jnp.int16),
        scratch_shapes=[pltpu.VMEM((4, HALF, LANES), jnp.float32)],
        compiler_params=pltpu.CompilerParams(vmem_limit_bytes=40 * 1024 * 1024),
        cost_estimate=pl.CostEstimate(flops=60 * slices * height * LANES, bytes_accessed=8 * slices * height * LANES, transcendentals=0),
        name="brick_right" if right else "brick_left",
    )(breakpoints, tf_color, tf_opacity, place, fields, halo, own)


def rim_kernel(slices, fields_ref, left_ref, right_ref):
    lane = lax.broadcasted_iota(jnp.int32, (2 * TILE, LANES), 1)
    rows = 2 * TILE

    def group(j, carry):
        base = pl.multiple_of(j * rows, rows)
        for f in range(4):
            for half, ref in ((0, left_ref), (1, right_ref)):
                total = jnp.zeros((rows, LANES), jnp.float32)
                for g in range(2):
                    for k in range(slices):
                        begin = g * 64 + k * 8
                        x = fields_ref[f, k, pl.ds(base + g * HALF, rows), half * LANES : (half + 1) * LANES]
                        x = pltpu.roll(x.astype(jnp.float32), (begin + 3) % LANES, 1)
                        total = jnp.where((lane >= begin) & (lane < begin + 8), x, total)
                ref[f, pl.ds(base, rows), :] = total.astype(ref.dtype)
        return carry

    lax.fori_loop(0, HALF // rows, group, 0)


def rims(fields):
    _, slices, height, width = fields.shape
    compact = pl.BlockSpec((4, HALF, LANES), lambda i: (0, i, 0))
    shape = jax.ShapeDtypeStruct((4, height // 2, LANES), jnp.bfloat16)
    return pl.pallas_call(
        functools.partial(rim_kernel, slices),
        grid=(height // BLOCK,),
        in_specs=[pl.BlockSpec((4, slices, BLOCK, width), lambda i: (0, 0, i, 0))],
        out_specs=[compact, compact],
        out_shape=[shape, shape],
        compiler_params=pltpu.CompilerParams(vmem_limit_bytes=40 * 1024 * 1024),
        cost_estimate=pl.CostEstimate(flops=4 * slices * height * width, bytes_accessed=8 * slices * height * width, transcendentals=0),
        name="rims",
    )(fields)


def image_kernel(count_x, count_z, order_ref, left_ref, right_ref, out_ref):
    lane = lax.broadcasted_iota(jnp.int32, (4 * TILE, LANES), 1)

    def decode(code):
        root = (code.astype(jnp.int32) + 32767).astype(jnp.float32) * (1.0 / CODE)
        return root * root

    def column(i, carry):
        image = [jnp.zeros((3 * TILE, LANES), jnp.float32) for _ in range(2)]
        through = [jnp.ones((TILE, LANES), jnp.float32) for _ in range(2)]
        for k in range(count_z):
            d = order_ref[i, k]
            turn = 3 * d
            own = i * count_z + d
            behind = jnp.maximum(i - 1, 0) * count_z + d
            left = pltpu.roll(decode(left_ref[own]), turn, 1)
            right = pltpu.roll(decode(right_ref[own]), turn, 1)
            before = jnp.where(i > 0, pltpu.roll(decode(right_ref[behind]), turn, 1), 0.0)
            pieces = (jnp.where(lane < turn, before, left), jnp.where(lane < turn, left, right))
            for side in range(2):
                piece = pieces[side]
                t = through[side]
                image[side] = image[side] + jnp.concatenate([t, t, t], axis=0) * piece[: 3 * TILE]
                through[side] = t * (1.0 - piece[3 * TILE :])
        for side in range(2):
            at = pl.multiple_of((2 * i + side) * LANES, LANES)
            for c in range(3):
                out_ref[c, :, pl.ds(at, LANES)] = image[side][c * TILE : (c + 1) * TILE]
            out_ref[3, :, pl.ds(at, LANES)] = 1.0 - through[side]
        return carry

    lax.fori_loop(0, count_x, column, 0)


def compose(order, left, right, count_x, count_z):
    vmem = pl.BlockSpec(memory_space=pltpu.VMEM)
    return pl.pallas_call(
        functools.partial(image_kernel, count_x, count_z),
        in_specs=[pl.BlockSpec(memory_space=pltpu.SMEM), vmem, vmem],
        out_specs=vmem,
        out_shape=jax.ShapeDtypeStruct((4, TILE, count_x * 2 * LANES), jnp.float32),
        compiler_params=pltpu.CompilerParams(vmem_limit_bytes=40 * 1024 * 1024),
        name="compose",
    )(order, left, right)


def per_device(fields, breakpoints, tf_color, tf_opacity, depth_order, live_rows):
    count_x, count_z = lax.axis_size("bx"), lax.axis_size("bz")
    here, depth = lax.axis_index("bx"), lax.axis_index("bz")
    live = live_rows.reshape(2)
    next_live = lax.ppermute(live, "bx", [(i + 1, i) for i in range(count_x - 1)])
    scalars = jnp.stack([(here > 0).astype(jnp.int32), live[0], live[1], next_live[0], next_live[1], LANES - 3 * depth])
    left_rim, right_rim = rims(fields)
    behind = lax.ppermute(right_rim, "bx", [(i, i + 1) for i in range(count_x - 1)])
    tf = (breakpoints, tf_color, tf_opacity, scalars)
    right = brick_half(True, *tf, fields, left_rim, right_rim)
    right = lax.all_to_all(right, ("bx", "bz"), split_axis=0, concat_axis=0, tiled=True)
    left = brick_half(False, *tf, fields, behind, left_rim)
    left = lax.all_to_all(left, ("bx", "bz"), split_axis=0, concat_axis=0, tiled=True)
    return compose(depth_order, left, right, count_x, count_z)


def solution(mesh):
    return jax.shard_map(
        per_device,
        mesh=mesh,
        in_specs=(P(None, "bz", None, "bx"), P(), P(), P(), P(), P("bx", "bz", None)),
        out_specs=P(None, ("bx", "bz"), None),
        check_vma=False,
    )
```

time: 490 us -> 163 us (0.33)
  other arithmetic: 273 us -> 0 us
  local copies, waits for them, and re-layouts: 101 us -> 2.88 us
  Pallas kernels: 0 us -> 93.9 us
  between operations: 43.6 us -> 0.08 us
  waiting for transfers between devices: 52.5 us -> 36.7 us
  starting transfers between devices: 15.3 us -> 29.3 us
    mul x47 -> x0, other arithmetic: 192 us -> none  [the longest x8 60.8 us: classify(): alpha * lookup(tf_color[:, 0])]
    pallas_call x0 -> x4, Pallas kernels: none -> 93.9 us  [the longest x2 78.5 us: brick_half(): pl.pallas_call(functools.partial(brick_kernel, slices, right), grid=(heig...]
    dynamic_slice x16 -> x0, local copies, waits for them, and re-layouts: 48.5 us -> none  [advance(): lax.dynamic_index_in_dim(fields, k, 1, keepdims=False)]
    add x13 -> x0, other arithmetic: 45.8 us -> none  [the longest x8 45.3 us: advance(): return acc + (1.0 - acc[3:4]) * ((1.0 - frac) * near + frac * far)]
    all_to_all x1 -> x2, waiting for transfers between devices: 52.5 us -> 18.8 us  [the longest x1 18.8 us: per_device(): lax.all_to_all(left, ('bx', 'bz'), split_axis=0, concat_axis=0, tiled=True)]
    slice x22 -> x1, local copies, waits for them, and re-layouts: 22.5 us -> 1.38 us  [per_device(): live[1]]
    while x8 -> x0, other arithmetic: 19.9 us -> none
    ppermute x1 -> x2, waiting for transfers between devices: 0.01 us -> 17.9 us  [the longest x1 17.8 us: per_device(): lax.ppermute(right_rim, 'bx', [(i, i + 1) for i in range(count_x - 1)])]
  transfers between devices with their start and end apart: 2 -> 4, of which waited for: 1 -> 2; matrix products, arithmetic and copies ran while one was open for 1% -> 1% of each run, Pallas kernels for 0% -> 31%
where the time goes in v1:
time: 163 us
  Pallas kernels  93.9 us (58%)
  waiting for transfers between devices  36.7 us (23%)
  starting transfers between devices  29.3 us (18%)
  local copies, waits for them, and re-layouts  2.88 us (2%)
    pallas_call x2, Pallas kernels, brick_half(): pl.pallas_call(functools.partial(brick_kernel, slices, right), grid=(heig...  78.5 us
    all_to_all x1, waiting for transfers between devices, per_device(): lax.all_to_all(left, ('bx', 'bz'), split_axis=0, concat_axis=0, tiled=True)  18.8 us
    ppermute x1, waiting for transfers between devices, per_device(): lax.ppermute(right_rim, 'bx', [(i, i + 1) for i in range(count_x - 1)])  17.8 us
    all_to_all x1, starting transfers between devices, per_device(): lax.all_to_all(right, ('bx', 'bz'), split_axis=0, concat_axis=0, tiled=True)  12.6 us
    all_to_all x1, starting transfers between devices, per_device(): lax.all_to_all(left, ('bx', 'bz'), split_axis=0, concat_axis=0, tiled=True)  12 us
    pallas_call x1, Pallas kernels, rims(): pl.pallas_call(functools.partial(rim_kernel, slices), grid=(height // BLO...  11.1 us
    pallas_call x1, Pallas kernels, compose(): pl.pallas_call(functools.partial(image_kernel, count_x, count_z), in_spec...  4.27 us
    ppermute x1, starting transfers between devices, per_device(): lax.ppermute(right_rim, 'bx', [(i, i + 1) for i in range(count_x - 1)])  3.32 us
  transfers between devices with their start and end apart: 4, of which 2 were waited for; matrix products, arithmetic and copies ran while one was open for 1% of the time, Pallas kernels for 31%

profile of v1, /device:TPU:1, one launch (start us, length us, event | category | flops | bytes accessed | tf_op | source)
XLA Modules:
  0.0 162.8 jit_solution(17934341411631799150)
XLA Ops:
  0.0 0.0 copy-start.3
  0.0 0.0 copy-start
  0.0 0.0 copy-start.1
  0.0 1.4 collective-permute-start
  1.4 1.4 fusion
  2.8 11.1 %rims.1 = (bf16[4,512,128]{2,1,0:T(8,128)(2,1)S(1)}, bf16[4,512,128]{2,1,0:T(8,128)(2,1)S(1)}) custom-call(bf16[4,8,1024,256]{3,2,1,0:T(8,128)(2,1)} %fields_ref.5), custom_call_target="tpu_custom_call" | custom-call | flops 8388608 | bytes 16777216 | tf_op jit(solution)/shard_map/rims/pallas_call | solution.py:209
  13.9 0.0 copy-done.3
  14.0 0.1 copy.7.color_ref
  14.0 0.0 collective-permute-done
  14.0 1.3 stack.15.place_ref
  15.4 0.0 copy-done
  15.4 0.0 copy-done.1
  15.4 0.0 copy-start.2
  15.4 39.3 %brick_right.1 = s16[128,32,128]{2,1,0:T(8,128)(2,1)} custom-call(s32[8]{0:T(128)S(1)} %copy-done, f32[8,3]{1,0:T(8,128)S(1)} %copy.7.color_ref, f32[8]{0:T(128)S(1)} %copy-done.1, s32[6]{0:T(128)S(1)} %stack.15.place_ref, bf16[4,8,1024,256]{3,2,1,0:T(8,128)(2,1)} %fields_ref.5, bf16[4,512,128]{2,1,0:T(8,128)(2,1)S(1)} %get-tuple-element.8.own_ref.halo_ref, ...), custom_call_target="tpu_custom_call" | custom-call | flops 62914560 | bytes 8388608 | tf_op jit(solution)/shard_map/brick_right/pallas_call | solution.py:171
  54.6 12.6 %all-to-all-start.1 = ((s16[128,32,128]{2,1,0:T(8,128)(2,1)}), s16[128,32,128]{2,1,0:T(8,128)(2,1)S(1)}, u32[]{:S(2)}, u32[]{:S(2)}) async-start(s16[128,32,128]{2,1,0:T(8,128)(2,1)} %brick_right.1), calls=%async_computation.1 | async-start | bytes 2097152 | tf_op jit(solution)/shard_map/all_to_all | solution.py:277
  67.3 3.3 %collective-permute-start.1 = (bf16[4,512,128]{2,1,0:T(8,128)(2,1)S(1)}, bf16[4,512,128]{2,1,0:T(8,128)(2,1)S(1)}, u32[]{:S(2)}, u32[]{:S(2)}) collective-permute-start(bf16[4,512,128]{2,1,0:T(8,128)(2,1)S(1)} %get-tuple-element.7.own_ref), channel_id=1, source_target_pairs={{0,8},{8,16},{16,24},{24,32},{32,40},{40,48},{48,56},{56,64},{64,7... | collective-permute-start | bytes 1572872 | tf_op jit(solution)/shard_map/ppermute | solution.py:274
  70.6 17.8 %collective-permute-done.1.halo_ref = bf16[4,512,128]{2,1,0:T(8,128)(2,1)S(1)} collective-permute-done((bf16[4,512,128]{2,1,0:T(8,128)(2,1)S(1)}, bf16[4,512,128]{2,1,0:T(8,128)(2,1)S(1)}, u32[]{:S(2)}, u32[]{:S(2)}) %collective-permute-start.1) | collective-permute-done | bytes 524320 | tf_op jit(solution)/shard_map/ppermute | solution.py:274
  88.5 39.2 %brick_left.1 = s16[128,32,128]{2,1,0:T(8,128)(2,1)} custom-call(s32[8]{0:T(128)S(1)} %copy-done, f32[8,3]{1,0:T(8,128)S(1)} %copy.7.color_ref, f32[8]{0:T(128)S(1)} %copy-done.1, s32[6]{0:T(128)S(1)} %stack.15.place_ref, bf16[4,8,1024,256]{3,2,1,0:T(8,128)(2,1)} %fields_ref.5, bf16[4,512,128]{2,1,0:T(8,128)(2,1)S(1)} %collective-permute-done.1.halo_ref, ...), custom_call_target="tpu_custom_call" | custom-call | flops 62914560 | bytes 8388608 | tf_op jit(solution)/shard_map/brick_left/pallas_call | solution.py:171
  127.7 0.0 all-to-all-done.1.right_ref
  127.7 12.0 %all-to-all-start = ((s16[128,32,128]{2,1,0:T(8,128)(2,1)}), s16[128,32,128]{2,1,0:T(8,128)(2,1)S(1)}, u32[]{:S(2)}, u32[]{:S(2)}) async-start(s16[128,32,128]{2,1,0:T(8,128)(2,1)} %brick_left.1), calls=%async_computation | async-start | bytes 2097152 | tf_op jit(solution)/shard_map/all_to_all | solution.py:279
  139.6 0.0 copy-done.2
  139.7 0.1 copy.9.order_ref
  139.7 18.8 %all-to-all-done.left_ref = s16[128,32,128]{2,1,0:T(8,128)(2,1)S(1)} async-done(((s16[128,32,128]{2,1,0:T(8,128)(2,1)}), s16[128,32,128]{2,1,0:T(8,128)(2,1)S(1)}, u32[]{:S(2)}, u32[]{:S(2)}) %all-to-all-start) | async-done | bytes 1048608 | tf_op jit(solution)/shard_map/all_to_all | solution.py:279
  158.6 4.3 %compose.1 = f32[4,8,4096]{2,1,0:T(8,128)} custom-call(s32[16,8]{1,0:T(8,128)S(1)} %copy.9.order_ref, s16[128,32,128]{2,1,0:T(8,128)(2,1)S(1)} %all-to-all-done.left_ref, s16[128,32,128]{2,1,0:T(8,128)(2,1)S(1)} %all-to-all-done.1.right_ref), custom_call_target="tpu_custom_call" | custom-call | tf_op jit(solution)/shard_map/compose/pallas_call | solution.py:257
Async XLA Ops:
  0.0 13.9 %copy-start.3 = (f32[8,3]{0,1:T(4,128)S(1)}, f32[8,3]{0,1:T(4,128)}, u32[]{:S(2)}) copy-start(f32[8,3]{0,1:T(4,128)} %param.8) | copy-start | bytes 292
  0.0 15.4 %copy-start = (s32[8]{0:T(128)S(1)}, s32[8]{0:T(128)}, u32[]{:S(2)}) copy-start(s32[8]{0:T(128)} %bp_ref.3) | copy-start | bytes 100
  0.0 15.4 %copy-start.1 = (f32[8]{0:T(128)S(1)}, f32[8]{0:T(128)}, u32[]{:S(2)}) copy-start(f32[8]{0:T(128)} %opacity_ref.3) | copy-start | bytes 100
  0.0 14.0 %collective-permute-start = (s32[2]{0:T(128)}, s32[2]{0:T(128)S(1)}, u32[]{:S(2)}, u32[]{:S(2)}) collective-permute-start(s32[2]{0:T(128)} %bitcast.5), channel_id=1, source_target_pairs={{8,0},{16,8},{24,16},{32,24},{40,32},{48,40},{56,48},{64,56},{72,6... | collective-permute-start | bytes 32 | tf_op jit(solution)/shard_map/ppermute | solution.py:271
  15.4 124.3 %copy-start.2 = (s32[16,8]{0,1:T(8,128)S(1)}, s32[16,8]{0,1:T(8,128)}, u32[]{:S(2)}) copy-start(s32[16,8]{0,1:T(8,128)} %param.10) | copy-start | bytes 1540
  54.6 73.0 %all-to-all-start.1 = ((s16[128,32,128]{2,1,0:T(8,128)(2,1)}), s16[128,32,128]{2,1,0:T(8,128)(2,1)S(1)}, u32[]{:S(2)}, u32[]{:S(2)}) async-start(s16[128,32,128]{2,1,0:T(8,128)(2,1)} %brick_right.1), calls=%async_computation.1 | async-start | bytes 2097152 | tf_op jit(solution)/shard_map/all_to_all | solution.py:277
  67.3 21.2 %collective-permute-start.1 = (bf16[4,512,128]{2,1,0:T(8,128)(2,1)S(1)}, bf16[4,512,128]{2,1,0:T(8,128)(2,1)S(1)}, u32[]{:S(2)}, u32[]{:S(2)}) collective-permute-start(bf16[4,512,128]{2,1,0:T(8,128)(2,1)S(1)} %get-tuple-element.7.own_ref), channel_id=1, source_target_pairs={{0,8},{8,16},{16,24},{24,32},{32,40},{40,48},{48,56},{56,64},{64,7... | collective-permute-start | bytes 1572872 | tf_op jit(solution)/shard_map/ppermute | solution.py:274
  127.7 30.9 %all-to-all-start = ((s16[128,32,128]{2,1,0:T(8,128)(2,1)}), s16[128,32,128]{2,1,0:T(8,128)(2,1)S(1)}, u32[]{:S(2)}, u32[]{:S(2)}) async-start(s16[128,32,128]{2,1,0:T(8,128)(2,1)} %brick_left.1), calls=%async_computation | async-start | bytes 2097152 | tf_op jit(solution)/shard_map/all_to_all | solution.py:279

commit v2 on v1

v2 whole, which is shorter than its diff:
```python
import functools

import jax
import jax.numpy as jnp
from jax import lax
from jax.experimental import pallas as pl
from jax.experimental.pallas import tpu as pltpu
from jax.sharding import PartitionSpec as P

NBP = 8
LANES = 128
TILE = 8
BLOCK = 256
HALF = BLOCK // 2
GROUP = 16
UNROLL = 2
CODE = 65534.0
LOG2E = 1.4426950408889634
LOOKUP = "gather"


def tables(bp_ref, color_ref, opacity_ref):
    marks = [bp_ref[j].astype(jnp.float32) * (1.0 / 127.5) - 1.0 for j in range(NBP)]
    values = [[color_ref[j, c] for j in range(NBP)] for c in range(3)]
    values.append([opacity_ref[j] for j in range(NBP)])
    row = lax.broadcasted_iota(jnp.int32, (TILE, LANES), 0)

    def by_segment(scalars):
        table = jnp.full((TILE, LANES), scalars[0], jnp.float32)
        for j in range(1, NBP - 1):
            table = jnp.where(row >= j, scalars[j], table)
        return table

    low = by_segment(marks[: NBP - 1])
    width = by_segment(marks[1:]) - low
    pairs = []
    for c, value in enumerate(values):
        start = by_segment(value[: NBP - 1])
        slope = (by_segment(value[1:]) - start) / width
        offset = start - slope * low
        if c == 3:
            slope, offset = -LOG2E * slope, -LOG2E * offset
        pairs.append((offset, slope))
    return marks, pairs


def classify(raw, marks, pairs):
    h = jnp.tanh(raw[0] * 0.5)
    swirl = raw[1] * raw[1] + raw[2] * raw[2] + (raw[3] * raw[3] + 0.25)
    index = jnp.zeros(h.shape, jnp.int32)
    for j in range(1, NBP - 1):
        index = jnp.where(h >= marks[j], j, index)
    looked = []
    for offset, slope in pairs:
        parts = []
        for r in range(0, h.shape[0], TILE):
            own = index[r : r + TILE]
            parts.append(
                jnp.take_along_axis(offset, own, axis=0, mode="promise_in_bounds")
                + jnp.take_along_axis(slope, own, axis=0, mode="promise_in_bounds") * h[r : r + TILE]
            )
        looked.append(parts[0] if len(parts) == 1 else jnp.concatenate(parts, axis=0))
    return looked[:3], jnp.exp2(looked[3] * swirl)


def steps(slices):
    return [(3 * k // 8, (3 * k % 8) / 8.0) for k in range(slices)]


def turned(pair, columns):
    if columns == 0:
        return pair
    moved = [pltpu.roll(p, columns % LANES, 1) for p in pair]
    lane = lax.broadcasted_iota(jnp.int32, pair[0].shape, 1)
    if columns > 0:
        return [moved[0], jnp.where(lane < columns, moved[0], moved[1])]
    return [jnp.where(lane >= LANES + columns, moved[1], moved[0]), moved[1]]


def encode(value):
    return (jnp.sqrt(value) * CODE + 0.5).astype(jnp.int32) - 32767


def boundary(halo_ref, own_ref, keep, marks, pairs, slices):
    lane = lax.broadcasted_iota(jnp.int32, (HALF, LANES), 1)
    slot = lax.rem(lane, 8)
    slab = lax.rem(lax.div(lane, 8), 8)
    raw = []
    for f in range(4):
        raw.append(jnp.where(slot < 3, halo_ref[f].astype(jnp.float32), own_ref[f].astype(jnp.float32)))
    color, through = classify(raw, marks, pairs)
    through = jnp.where((slot < 3) & (keep == 0), 1.0, through)
    alpha = 1.0 - through
    samples = [alpha * c for c in color] + [through]
    whole = lax.div(3 * slab, 8)
    frac = lax.rem(3 * slab, 8).astype(jnp.float32) * 0.125
    sheared = [jnp.zeros((HALF, LANES), jnp.float32)] * 4
    for s in range(steps(slices)[-1][0] + 2):
        weight = jnp.where(whole == s, 1.0 - frac, 0.0) + jnp.where(whole + 1 == s, frac, 0.0)
        for c in range(4):
            moved = samples[c] if s == 0 else pltpu.roll(samples[c], s, 1)
            sheared[c] = sheared[c] + weight * moved
    product = sheared[3]
    for s in (1, 2, 4):
        product = product * jnp.where(slab >= s, pltpu.roll(product, 8 * s, 1), 1.0)
    before = jnp.where(slab >= 1, pltpu.roll(product, 8, 1), 1.0)
    result = []
    for c in range(3):
        total = before * sheared[c]
        for s in (1, 2, 4):
            total = total + jnp.where(slab >= s, pltpu.roll(total, 8 * s, 1), 0.0)
        result.append(total)
    return result + [1.0 - product]


def edge_kernel(slices, bp_ref, color_ref, opacity_ref, place_ref, halo_ref, own_ref, codes_ref, out_ref, edge_ref):
    marks, pairs = tables(bp_ref, color_ref, opacity_ref)
    lane = lax.broadcasted_iota(jnp.int32, (HALF, LANES), 1)
    row = lax.broadcasted_iota(jnp.int32, (HALF, LANES), 0) + pl.program_id(0) * BLOCK + jnp.where(lane < 64, 0, HALF)
    live = (row >= place_ref[1]) & (row < place_ref[2])
    for c, value in enumerate(boundary(halo_ref, own_ref, place_ref[0], marks, pairs, slices)):
        edge_ref[c] = encode(jnp.where(live, jnp.maximum(value, 0.0), 0.0))
    lane = lax.broadcasted_iota(jnp.int32, (4 * TILE, LANES), 1)
    for g in range(2):
        turn = (2 * LANES - (64 * g + 8 * (slices - 1) + 3)) % LANES
        for t in range(HALF // TILE):
            tile = g * (HALF // TILE) + t
            edge = jnp.concatenate([edge_ref[c, t * TILE : (t + 1) * TILE, :] for c in range(4)], axis=0)
            codes = jnp.where(lane < 3, pltpu.roll(edge, turn, 1), codes_ref[tile].astype(jnp.int32))
            out_ref[tile] = codes.astype(jnp.int16)


def with_edges(slices, breakpoints, tf_color, tf_opacity, place, halo, own, codes):
    smem = pl.BlockSpec(memory_space=pltpu.SMEM)
    compact = pl.BlockSpec((4, HALF, LANES), lambda i: (0, i, 0))
    first = pl.BlockSpec((BLOCK // TILE, 4 * TILE, LANES), lambda i: (i, 0, 0))
    return pl.pallas_call(
        functools.partial(edge_kernel, slices),
        grid=(codes.shape[0] * TILE // BLOCK,),
        in_specs=[smem, smem, smem, smem, compact, compact, first],
        out_specs=first,
        out_shape=jax.ShapeDtypeStruct(codes.shape, codes.dtype),
        scratch_shapes=[pltpu.VMEM((4, HALF, LANES), jnp.int32)],
        input_output_aliases={6: 0},
        compiler_params=pltpu.CompilerParams(vmem_limit_bytes=40 * 1024 * 1024),
        name="edges",
    )(breakpoints, tf_color, tf_opacity, place, halo, own, codes)


def brick_kernel(slices, bp_ref, color_ref, opacity_ref, place_ref, fields_ref, out_ref):
    marks, pairs = tables(bp_ref, color_ref, opacity_ref)
    plan = steps(slices)
    first = pl.program_id(0) * BLOCK
    rows = GROUP

    def group(j, carry):
        base = pl.multiple_of(j * rows, rows)
        sums = {}

        def add(s, weight, color):
            for c in range(3):
                terms = [w * q[c] for w, q in zip(weight, color)]
                sums[s, c] = [p + q for p, q in zip(sums[s, c], terms)] if (s, c) in sums else terms

        through = None
        for k in range(slices):
            whole, frac = plan[k]
            color, clear = [], []
            for side in range(2):
                raw = [
                    fields_ref[f, k, pl.ds(base, rows), side * LANES : (side + 1) * LANES].astype(jnp.float32) for f in range(4)
                ]
                some, clean = classify(raw, marks, pairs)
                color.append(some)
                clear.append(clean)
            alpha = [1.0 - c for c in clear]
            if through is None:
                add(0, alpha, color)
                through = clear
                continue
            near = [t * (1.0 - frac) for t in through] if frac else through
            add(whole, [w * a for w, a in zip(turned(near, -whole), alpha)], color)
            after = [n * c for n, c in zip(near, turned(clear, whole))]
            if frac:
                far = [t * frac for t in through]
                add(whole + 1, [w * a for w, a in zip(turned(far, -whole - 1), alpha)], color)
                after = [p + n * c for p, n, c in zip(after, far, turned(clear, whole + 1))]
            through = after
        reach = plan[-1][0] + 2
        done = []
        for c in range(3):
            moved = [turned(sums[s, c], s) for s in range(reach)]
            done.append([sum(m[side] for m in moved) for side in range(2)])
        done.append([1.0 - t for t in through])
        lane = lax.broadcasted_iota(jnp.int32, (TILE, LANES), 1)
        for r in range(rows // TILE):
            tile = (rows // TILE) * j + r
            row = lax.broadcasted_iota(jnp.int32, (TILE, LANES), 0) + (first + tile * TILE)
            live = [(row >= place_ref[1]) & (row < place_ref[2])]
            inside = lane < place_ref[5]
            live.append((row >= jnp.where(inside, place_ref[1], place_ref[3])) & (row < jnp.where(inside, place_ref[2], place_ref[4])))
            for side in range(2):
                codes = []
                for c in range(4):
                    value = done[c][side][r * TILE : (r + 1) * TILE]
                    codes.append(encode(jnp.where(live[side], jnp.maximum(value, 0.0), 0.0)))
                out_ref[tile, :, side * LANES : (side + 1) * LANES] = jnp.concatenate(codes, axis=0).astype(jnp.int16)
        return carry

    lax.fori_loop(0, BLOCK // rows, group, 0, unroll=UNROLL)


def brick(breakpoints, tf_color, tf_opacity, place, fields):
    _, slices, height, width = fields.shape
    smem = pl.BlockSpec(memory_space=pltpu.SMEM)
    return pl.pallas_call(
        functools.partial(brick_kernel, slices),
        grid=(height // BLOCK,),
        in_specs=[smem, smem, smem, smem, pl.BlockSpec((4, slices, BLOCK, width), lambda i: (0, 0, i, 0))],
        out_specs=pl.BlockSpec((BLOCK // TILE, 4 * TILE, width), lambda i: (i, 0, 0)),
        out_shape=jax.ShapeDtypeStruct((height // TILE, 4 * TILE, width), jnp.int16),
        compiler_params=pltpu.CompilerParams(vmem_limit_bytes=40 * 1024 * 1024),
        cost_estimate=pl.CostEstimate(flops=60 * slices * height * width, bytes_accessed=8 * slices * height * width, transcendentals=0),
        name="brick",
    )(breakpoints, tf_color, tf_opacity, place, fields)


def rim_kernel(slices, fields_ref, rim_ref):
    rows = 2 * TILE
    lane = lax.broadcasted_iota(jnp.int32, (rows, LANES), 1)

    def group(j, carry):
        base = pl.multiple_of(j * rows, rows)
        for f in range(4):
            total = jnp.zeros((rows, LANES), jnp.float32)
            for g in range(2):
                for k in range(slices):
                    begin = g * 64 + k * 8
                    left = fields_ref[f, k, pl.ds(base + g * HALF, rows), :LANES].astype(jnp.float32)
                    right = fields_ref[f, k, pl.ds(base + g * HALF, rows), LANES:].astype(jnp.float32)
                    both = pltpu.roll(jnp.where(lane < 64, left, right), (begin + 3) % LANES, 1)
                    total = jnp.where((lane >= begin) & (lane < begin + 8), both, total)
            rim_ref[f, pl.ds(base, rows), :] = total.astype(rim_ref.dtype)
        return carry

    lax.fori_loop(0, HALF // rows, group, 0)


def rims(fields):
    _, slices, height, width = fields.shape
    compact = pl.BlockSpec((4, HALF, LANES), lambda i: (0, i, 0))
    return pl.pallas_call(
        functools.partial(rim_kernel, slices),
        grid=(height // BLOCK,),
        in_specs=[pl.BlockSpec((4, slices, BLOCK, width), lambda i: (0, 0, i, 0))],
        out_specs=compact,
        out_shape=jax.ShapeDtypeStruct((4, height // 2, LANES), jnp.bfloat16),
        compiler_params=pltpu.CompilerParams(vmem_limit_bytes=40 * 1024 * 1024),
        cost_estimate=pl.CostEstimate(flops=4 * slices * height * width, bytes_accessed=8 * slices * height * width, transcendentals=0),
        name="rims",
    )(fields)


def image_kernel(count_x, count_z, order_ref, codes_ref, out_ref):
    lane = lax.broadcasted_iota(jnp.int32, (4 * TILE, LANES), 1)

    def decode(code):
        root = (code.astype(jnp.int32) + 32767).astype(jnp.float32) * (1.0 / CODE)
        return root * root

    def column(i, carry):
        image = [jnp.zeros((3 * TILE, LANES), jnp.float32) for _ in range(2)]
        through = [jnp.ones((TILE, LANES), jnp.float32) for _ in range(2)]
        for k in range(count_z):
            d = order_ref[i, k]
            turn = 3 * d
            own = i * count_z + d
            behind = jnp.maximum(i - 1, 0) * count_z + d
            left = pltpu.roll(decode(codes_ref[own, :, :LANES]), turn, 1)
            right = pltpu.roll(decode(codes_ref[own, :, LANES:]), turn, 1)
            before = jnp.where(i > 0, pltpu.roll(decode(codes_ref[behind, :, LANES:]), turn, 1), 0.0)
            pieces = (jnp.where(lane < turn, before, left), jnp.where(lane < turn, left, right))
            for side in range(2):
                piece = pieces[side]
                t = through[side]
                image[side] = image[side] + jnp.concatenate([t, t, t], axis=0) * piece[: 3 * TILE]
                through[side] = t * (1.0 - piece[3 * TILE :])
        for side in range(2):
            at = pl.multiple_of((2 * i + side) * LANES, LANES)
            for c in range(3):
                out_ref[c, :, pl.ds(at, LANES)] = image[side][c * TILE : (c + 1) * TILE]
            out_ref[3, :, pl.ds(at, LANES)] = 1.0 - through[side]
        return carry

    lax.fori_loop(0, count_x, column, 0)


def compose(order, codes, count_x, count_z):
    vmem = pl.BlockSpec(memory_space=pltpu.VMEM)
    return pl.pallas_call(
        functools.partial(image_kernel, count_x, count_z),
        in_specs=[pl.BlockSpec(memory_space=pltpu.SMEM), vmem],
        out_specs=vmem,
        out_shape=jax.ShapeDtypeStruct((4, TILE, count_x * 2 * LANES), jnp.float32),
        compiler_params=pltpu.CompilerParams(vmem_limit_bytes=40 * 1024 * 1024),
        name="compose",
    )(order, codes)


def per_device(fields, breakpoints, tf_color, tf_opacity, depth_order, live_rows):
    count_x, count_z = lax.axis_size("bx"), lax.axis_size("bz")
    here, depth = lax.axis_index("bx"), lax.axis_index("bz")
    live = live_rows.reshape(2)
    next_live = lax.ppermute(live, "bx", [(i + 1, i) for i in range(count_x - 1)])
    scalars = jnp.stack([(here > 0).astype(jnp.int32), live[0], live[1], next_live[0], next_live[1], LANES - 3 * depth])
    rim = rims(fields)
    behind = lax.ppermute(rim, "bx", [(i, i + 1) for i in range(count_x - 1)])
    tf = (breakpoints, tf_color, tf_opacity, scalars)
    codes = with_edges(fields.shape[1], *tf, behind, rim, brick(*tf, fields))
    codes = lax.all_to_all(codes, ("bx", "bz"), split_axis=0, concat_axis=0, tiled=True)
    return compose(depth_order, codes, count_x, count_z)


def solution(mesh):
    return jax.shard_map(
        per_device,
        mesh=mesh,
        in_specs=(P(None, "bz", None, "bx"), P(), P(), P(), P(), P("bx", "bz", None)),
        out_specs=P(None, ("bx", "bz"), None),
        check_vma=False,
    )
```

time: 163 us -> 99.3 us (0.61)
  Pallas kernels: 93.9 us -> 45 us
  starting transfers between devices: 29.3 us -> 19.1 us
  waiting for transfers between devices: 36.7 us -> 32.7 us
    pallas_call x2, Pallas kernels: 78.5 us -> 32.5 us  [the longest x1 26.1 us: brick(): pl.pallas_call(functools.partial(brick_kernel, slices), grid=(height // B...]
    ppermute x1, waiting for transfers between devices: 17.8 us -> 0.01 us  [per_device(): behind = lax.ppermute(rim, 'bx', [(i, i + 1) for i in range(count_x - 1)])]
    all_to_all x2 -> x1, waiting for transfers between devices: 18.8 us -> 30.4 us  [per_device(): lax.all_to_all(codes, ('bx', 'bz'), split_axis=0, concat_axis=0, tiled=True)]
    all_to_all x2 -> x1, starting transfers between devices: 24.6 us -> 13.8 us  [per_device(): lax.all_to_all(codes, ('bx', 'bz'), split_axis=0, concat_axis=0, tiled=True)]
    pallas_call x1, Pallas kernels: 11.1 us -> 8.24 us  [rims(): pl.pallas_call(functools.partial(rim_kernel, slices), grid=(height // BLO...]
    ppermute x1, waiting for transfers between devices: 0.01 us -> 2.25 us  [per_device(): lax.ppermute(live, 'bx', [(i + 1, i) for i in range(count_x - 1)])]
  transfers between devices with their start and end apart: 4 -> 3, of which waited for: 2 -> 2; matrix products, arithmetic and copies ran while one was open for 1% -> 2% of each run, Pallas kernels for 31% -> 26%
where the time goes in v2:
time: 99.3 us; the launch traced here: 99 us
  Pallas kernels  45 us (45%)
  waiting for transfers between devices  32.7 us (33%)
  starting transfers between devices  19.1 us (19%)
  local copies, waits for them, and re-layouts  2.14 us (2%)
    all_to_all x1, waiting for transfers between devices, per_device(): lax.all_to_all(codes, ('bx', 'bz'), split_axis=0, concat_axis=0, tiled=True)  30.4 us
    pallas_call x1, Pallas kernels, brick(): pl.pallas_call(functools.partial(brick_kernel, slices), grid=(height // B...  26.1 us
    all_to_all x1, starting transfers between devices, per_device(): lax.all_to_all(codes, ('bx', 'bz'), split_axis=0, concat_axis=0, tiled=True)  13.8 us
    pallas_call x1, Pallas kernels, rims(): pl.pallas_call(functools.partial(rim_kernel, slices), grid=(height // BLO...  8.24 us
    pallas_call x1, Pallas kernels, with_edges(): pl.pallas_call(functools.partial(edge_kernel, slices), grid=(codes.shape[...  6.39 us
    pallas_call x1, Pallas kernels, compose(): pl.pallas_call(functools.partial(image_kernel, count_x, count_z), in_spec...  4.27 us
    ppermute x1, starting transfers between devices, per_device(): behind = lax.ppermute(rim, 'bx', [(i, i + 1) for i in range(count_x - 1)])  3.98 us
    ppermute x1, waiting for transfers between devices, per_device(): lax.ppermute(live, 'bx', [(i + 1, i) for i in range(count_x - 1)])  2.25 us
  transfers between devices with their start and end apart: 3, of which 2 were waited for; matrix products, arithmetic and copies ran while one was open for 2% of the time, Pallas kernels for 26%

profile of v2, /device:TPU:1, one launch (start us, length us, event | category | flops | bytes accessed | tf_op | source)
XLA Modules:
  0.0 99.0 jit_solution(16096908445961141914)
XLA Ops:
  0.0 0.0 copy-start.4
  0.0 0.0 copy-start.3
  0.0 0.0 copy-start
  0.0 0.0 copy-start.1
  0.0 8.2 %rims.1.own_ref = bf16[4,512,128]{2,1,0:T(8,128)(2,1)S(1)} custom-call(bf16[4,8,1024,256]{3,2,1,0:T(8,128)(2,1)} %fields_ref.3), custom_call_target="tpu_custom_call" | custom-call | flops 8388608 | bytes 16777216 | tf_op jit(solution)/shard_map/rims/pallas_call | solution.py:252
  8.3 4.0 %collective-permute-start.1 = (bf16[4,512,128]{2,1,0:T(8,128)(2,1)S(1)}, bf16[4,512,128]{2,1,0:T(8,128)(2,1)S(1)}, u32[]{:S(2)}, u32[]{:S(2)}) collective-permute-start(bf16[4,512,128]{2,1,0:T(8,128)(2,1)S(1)} %rims.1.own_ref), channel_id=1, source_target_pairs={{0,8},{8,16},{16,24},{24,32},{32,40},{40,48},{48,56},{56,64},{64,7... | collective-permute-start | bytes 1572872 | tf_op jit(solution)/shard_map/ppermute | solution.py:317
  12.3 0.0 copy-done.4
  12.3 1.3 %collective-permute-start = (s32[2]{0:T(128)S(1)}, s32[2]{0:T(128)S(1)}, u32[]{:S(2)}, u32[]{:S(2)}) collective-permute-start(s32[2]{0:T(128)S(1)} %bitcast.5), channel_id=1, source_target_pairs={{8,0},{16,8},{24,16},{32,24},{40,32},{48,40},{56,48},{64,56},{72,6... | collective-permute-start | bytes 32 | tf_op jit(solution)/shard_map/ppermute | solution.py:314
  13.6 0.0 copy-done.3
  13.6 0.1 copy.9.color_ref
  13.7 0.6 fusion
  14.3 2.3 %collective-permute-done = s32[2]{0:T(128)S(1)} collective-permute-done((s32[2]{0:T(128)S(1)}, s32[2]{0:T(128)S(1)}, u32[]{:S(2)}, u32[]{:S(2)}) %collective-permute-start) | collective-permute-done | bytes 40 | tf_op jit(solution)/shard_map/ppermute | solution.py:314
  16.5 1.3 %stack.15.place_ref = s32[6]{0:T(128)S(1)} concatenate(s32[1]{0:T(128)} %bitcast, s32[1]{0:T(128)} %bitcast.1, s32[1]{0:T(128)} %bitcast.2, s32[2]{0:T(128)S(1)} %collective-permute-done, s32[1]{0:T(128)} %bitcast.4), dimensions={0} | concatenate | bytes 48 | tf_op jit(solution)/shard_map/stack | solution.py:315
  17.9 0.0 copy-done
  17.9 0.0 copy-done.1
  17.9 26.1 %brick.1.codes_ref = s16[128,32,256]{2,1,0:T(8,128)(2,1)} custom-call(s32[8]{0:T(128)S(1)} %copy-done, f32[8,3]{1,0:T(8,128)S(1)} %copy.9.color_ref, f32[8]{0:T(128)S(1)} %copy-done.1, s32[6]{0:T(128)S(1)} %stack.15.place_ref, bf16[4,8,1024,256]{3,2,1,0:T(8,128)(2,1)} %fields_ref.3), custom_call_target="tpu_custom_call" | custom-call | flops 125829120 | bytes 16777216 | tf_op jit(solution)/shard_map/brick/pallas_call | solution.py:216
  44.0 0.0 collective-permute-done.1.halo_ref
  44.0 6.4 %edges.1 = s16[128,32,256]{2,1,0:T(8,128)(2,1)} custom-call(s32[8]{0:T(128)S(1)} %copy-done, f32[8,3]{1,0:T(8,128)S(1)} %copy.9.color_ref, f32[8]{0:T(128)S(1)} %copy-done.1, s32[6]{0:T(128)S(1)} %stack.15.place_ref, bf16[4,512,128]{2,1,0:T(8,128)(2,1)S(1)} %collective-permute-done.1.halo_ref, ...), custom_call_target="tpu_custom_call", output_to_operand_aliasing={{}: (6, {})} | custom-call | tf_op jit(solution)/shard_map/edges/pallas_call | solution.py:137
  50.4 0.0 copy-start.2
  50.4 13.8 %all-to-all-start = ((s16[128,32,256]{2,1,0:T(8,128)(2,1)}), s16[128,32,256]{2,1,0:T(8,128)(2,1)S(1)}, u32[]{:S(2)}, u32[]{:S(2)}) async-start(s16[128,32,256]{2,1,0:T(8,128)(2,1)} %edges.1), calls=%async_computation | async-start | bytes 4194304 | tf_op jit(solution)/shard_map/all_to_all | solution.py:320
  64.2 0.0 copy-done.2
  64.2 0.1 copy.10.order_ref
  64.3 30.4 %all-to-all-done.codes_ref = s16[128,32,256]{2,1,0:T(8,128)(2,1)S(1)} async-done(((s16[128,32,256]{2,1,0:T(8,128)(2,1)}), s16[128,32,256]{2,1,0:T(8,128)(2,1)S(1)}, u32[]{:S(2)}, u32[]{:S(2)}) %all-to-all-start) | async-done | bytes 2097184 | tf_op jit(solution)/shard_map/all_to_all | solution.py:320
  94.7 4.3 %compose.1 = f32[4,8,4096]{2,1,0:T(8,128)} custom-call(s32[16,8]{1,0:T(8,128)S(1)} %copy.10.order_ref, s16[128,32,256]{2,1,0:T(8,128)(2,1)S(1)} %all-to-all-done.codes_ref), custom_call_target="tpu_custom_call" | custom-call | tf_op jit(solution)/shard_map/compose/pallas_call | solution.py:300
Async XLA Ops:
  0.0 12.3 %copy-start.4 = (s32[1,1,2]{2,1,0:T(1,128)S(1)}, s32[1,1,2]{2,1,0:T(1,128)}, u32[]{:S(2)}) copy-start(s32[1,1,2]{2,1,0:T(1,128)} %param.11) | copy-start | bytes 28
  0.0 13.6 %copy-start.3 = (f32[8,3]{0,1:T(4,128)S(1)}, f32[8,3]{0,1:T(4,128)}, u32[]{:S(2)}) copy-start(f32[8,3]{0,1:T(4,128)} %param.8) | copy-start | bytes 292
  0.0 17.9 %copy-start = (s32[8]{0:T(128)S(1)}, s32[8]{0:T(128)}, u32[]{:S(2)}) copy-start(s32[8]{0:T(128)} %bp_ref.3) | copy-start | bytes 100
  0.0 17.9 %copy-start.1 = (f32[8]{0:T(128)S(1)}, f32[8]{0:T(128)}, u32[]{:S(2)}) copy-start(f32[8]{0:T(128)} %opacity_ref.3) | copy-start | bytes 100
  8.3 35.8 %collective-permute-start.1 = (bf16[4,512,128]{2,1,0:T(8,128)(2,1)S(1)}, bf16[4,512,128]{2,1,0:T(8,128)(2,1)S(1)}, u32[]{:S(2)}, u32[]{:S(2)}) collective-permute-start(bf16[4,512,128]{2,1,0:T(8,128)(2,1)S(1)} %rims.1.own_ref), channel_id=1, source_target_pairs={{0,8},{8,16},{16,24},{24,32},{32,40},{40,48},{48,56},{56,64},{64,7... | collective-permute-start | bytes 1572872 | tf_op jit(solution)/shard_map/ppermute | solution.py:317
  12.3 4.3 %collective-permute-start = (s32[2]{0:T(128)S(1)}, s32[2]{0:T(128)S(1)}, u32[]{:S(2)}, u32[]{:S(2)}) collective-permute-start(s32[2]{0:T(128)S(1)} %bitcast.5), channel_id=1, source_target_pairs={{8,0},{16,8},{24,16},{32,24},{40,32},{48,40},{56,48},{64,56},{72,6... | collective-permute-start | bytes 32 | tf_op jit(solution)/shard_map/ppermute | solution.py:314
  50.4 13.8 %copy-start.2 = (s32[16,8]{0,1:T(8,128)S(1)}, s32[16,8]{0,1:T(8,128)}, u32[]{:S(2)}) copy-start(s32[16,8]{0,1:T(8,128)} %param.10) | copy-start | bytes 1540
  50.4 44.3 %all-to-all-start = ((s16[128,32,256]{2,1,0:T(8,128)(2,1)}), s16[128,32,256]{2,1,0:T(8,128)(2,1)S(1)}, u32[]{:S(2)}, u32[]{:S(2)}) async-start(s16[128,32,256]{2,1,0:T(8,128)(2,1)} %edges.1), calls=%async_computation | async-start | bytes 4194304 | tf_op jit(solution)/shard_map/all_to_all | solution.py:320

commit v3 on v2

v3 whole, which is shorter than its diff:
```python
import functools

import jax
import jax.numpy as jnp
from jax import lax
from jax.experimental import pallas as pl
from jax.experimental.pallas import tpu as pltpu
from jax.sharding import PartitionSpec as P

NBP = 8
LANES = 128
TILE = 8
BLOCK = 128
HALF = BLOCK // 2
GROUP = 16
SUB = GROUP // 2
UNROLL = 2
EDGES = 512
COLUMNS = 1
PATCH = 4
DEPTHS = 8
CODE = 32767.0
LOG2E = 1.4426950408889634


def tables(bp_ref, color_ref, opacity_ref):
    marks = [bp_ref[j].astype(jnp.float32) * (1.0 / 127.5) - 1.0 for j in range(NBP)]
    values = [[color_ref[j, c] for j in range(NBP)] for c in range(3)]
    values.append([opacity_ref[j] for j in range(NBP)])
    row = lax.broadcasted_iota(jnp.int32, (TILE, LANES), 0)

    def by_segment(scalars):
        table = jnp.full((TILE, LANES), scalars[0], jnp.float32)
        for j in range(1, NBP - 1):
            table = jnp.where(row >= j, scalars[j], table)
        return table

    low = by_segment(marks[: NBP - 1])
    width = by_segment(marks[1:]) - low
    pairs = []
    for c, value in enumerate(values):
        if c < 3:
            value = [v * (CODE * CODE) for v in value]
        start = by_segment(value[: NBP - 1])
        slope = (by_segment(value[1:]) - start) / width
        offset = start - slope * low
        if c == 3:
            slope, offset = -LOG2E * slope, -LOG2E * offset
        pairs.append((offset, slope))
    return marks, (by_segment(marks[1 : NBP - 1] + [2.0]), pairs)


def looked_up(table, index):
    return jnp.take_along_axis(table, index, axis=0, mode="promise_in_bounds")


def classify(raw, marks, pairs):
    h = jnp.tanh(raw[0] * 0.5)
    swirl = raw[1] * raw[1] + raw[2] * raw[2] + (raw[3] * raw[3] + 0.25)
    index = jnp.zeros(h.shape, jnp.int32)
    for j in range(2, NBP - 1, 2):
        index = jnp.where(h >= marks[j], j, index)
    between, pairs = pairs
    parts = []
    for r in range(0, h.shape[0], TILE):
        segment, level = index[r : r + TILE], h[r : r + TILE]
        segment = jnp.where(level >= looked_up(between, segment), segment + 1, segment)
        parts.append([looked_up(offset, segment) + looked_up(slope, segment) * level for offset, slope in pairs])
    looked = [p[0] if len(p) == 1 else jnp.concatenate(p, axis=0) for p in zip(*parts)]
    return looked[:3], jnp.exp2(looked[3] * swirl)


def steps(slices):
    return [(3 * k // 8, (3 * k % 8) / 8.0) for k in range(slices)]


def turned(pair, columns):
    if columns == 0:
        return pair
    moved = [pltpu.roll(p, columns % LANES, 1) for p in pair]
    lane = lax.broadcasted_iota(jnp.int32, pair[0].shape, 1)
    if columns > 0:
        return [moved[0], jnp.where(lane < columns, moved[0], moved[1])]
    return [jnp.where(lane >= LANES + columns, moved[1], moved[0]), moved[1]]


def encode(value, live):
    code = (value * lax.rsqrt(value) + 0.5).astype(jnp.int32)
    return jnp.where(live, code, -1)


def boundary(halo, own, keep, marks, pairs, slices):
    lane = lax.broadcasted_iota(jnp.int32, (EDGES, LANES), 1)
    slot = lax.rem(lane, 8)
    slab = lax.rem(lax.div(lane, 8), 8)
    raw = []
    for f in range(4):
        raw.append(jnp.where(slot < 3, halo[f].astype(jnp.float32), own[f].astype(jnp.float32)))
    color, through = classify(raw, marks, pairs)
    through = jnp.where((slot < 3) & (keep == 0), 1.0, through)
    alpha = 1.0 - through
    samples = [alpha * c for c in color] + [through]
    whole = lax.div(3 * slab, 8)
    frac = lax.rem(3 * slab, 8).astype(jnp.float32) * 0.125
    sheared = [jnp.zeros((EDGES, LANES), jnp.float32)] * 4
    for s in range(steps(slices)[-1][0] + 2):
        weight = jnp.where(whole == s, 1.0 - frac, 0.0) + jnp.where(whole + 1 == s, frac, 0.0)
        for c in range(4):
            moved = samples[c] if s == 0 else pltpu.roll(samples[c], s, 1)
            sheared[c] = sheared[c] + weight * moved
    product = sheared[3]
    for s in (1, 2, 4):
        product = product * jnp.where(slab >= s, pltpu.roll(product, 8 * s, 1), 1.0)
    before = jnp.where(slab >= 1, pltpu.roll(product, 8, 1), 1.0)
    result = []
    for c in range(3):
        total = before * sheared[c]
        for s in (1, 2, 4):
            total = total + jnp.where(slab >= s, pltpu.roll(total, 8 * s, 1), 0.0)
        result.append(total)
    return result + [CODE * CODE - CODE * CODE * product]


def edge_kernel(slices, bp_ref, color_ref, opacity_ref, live_ref, halo_ref, own_ref, codes_ref, out_ref, edge_ref):
    marks, pairs = tables(bp_ref, color_ref, opacity_ref)
    has_left = lax.axis_index("bx")
    lane = lax.broadcasted_iota(jnp.int32, (EDGES, LANES), 1)
    line = lax.broadcasted_iota(jnp.int32, (EDGES, LANES), 0)
    line = line + lax.div(line, SUB) * SUB + jnp.where(lane < 64, 0, SUB)
    for part in range(halo_ref.shape[1] // EDGES):
        rows = slice(part * EDGES, (part + 1) * EDGES)
        live = (line + 2 * EDGES * part >= live_ref[0]) & (line + 2 * EDGES * part < live_ref[1])
        halo, own = halo_ref[:, rows, :], own_ref[:, rows, :]
        for c, value in enumerate(boundary(halo, own, has_left, marks, pairs, slices)):
            edge_ref[c, rows, :] = encode(value, live)
    lane = lax.broadcasted_iota(jnp.int32, (4 * TILE, LANES), 1)
    count = SUB // TILE

    def patch(j, carry):
        for g in range(2):
            turn = (2 * LANES - (64 * g + 8 * (slices - 1) + 3)) % LANES
            for t in range(count):
                tile = (2 * j + g) * count + t
                at = pl.ds(pl.multiple_of((j * count + t) * TILE, TILE), TILE)
                edge = jnp.concatenate([edge_ref[c, at, :] for c in range(4)], axis=0)
                codes = jnp.where(lane < 3, pltpu.roll(edge, turn, 1), codes_ref[tile, :, :LANES].astype(jnp.int32))
                out_ref[tile, :, :LANES] = codes.astype(jnp.int16)
                out_ref[tile, :, LANES:] = codes_ref[tile, :, LANES:]
        return carry

    lax.fori_loop(0, codes_ref.shape[0] // (2 * count), patch, 0, unroll=PATCH)


def with_edges(slices, breakpoints, tf_color, tf_opacity, live, halo, own, codes):
    smem = pl.BlockSpec(memory_space=pltpu.SMEM)
    vmem = pl.BlockSpec(memory_space=pltpu.VMEM)
    return pl.pallas_call(
        functools.partial(edge_kernel, slices),
        in_specs=[smem, smem, smem, smem, vmem, vmem, vmem],
        out_specs=vmem,
        out_shape=jax.ShapeDtypeStruct(codes.shape, codes.dtype),
        scratch_shapes=[pltpu.VMEM((4, halo.shape[1], LANES), jnp.int32)],
        compiler_params=pltpu.CompilerParams(vmem_limit_bytes=40 * 1024 * 1024),
        name="edges",
    )(breakpoints, tf_color, tf_opacity, live, halo, own, codes)


def brick_kernel(slices, bp_ref, color_ref, opacity_ref, live_ref, fields_ref, out_ref, rim_ref, packed_ref):
    marks, pairs = tables(bp_ref, color_ref, opacity_ref)
    plan = steps(slices)
    first = pl.program_id(0) * BLOCK
    rows = GROUP
    wide = lax.broadcasted_iota(jnp.int32, (SUB, LANES), 1)
    own_columns = LANES - 3 * lax.axis_index("bz")

    def group(j, carry):
        base = pl.multiple_of(j * rows, rows)
        spot = pl.ds(pl.multiple_of(j * SUB, SUB), SUB)
        sums = {}

        def add(s, weight, color):
            for c in range(3):
                terms = [w * q[c] for w, q in zip(weight, color)]
                sums[s, c] = [p + q for p, q in zip(sums[s, c], terms)] if (s, c) in sums else terms

        through = None
        for k in range(slices):
            whole, frac = plan[k]
            color, clear, raws = [], [], []
            for side in range(2):
                raw = [
                    fields_ref[f, k, pl.ds(base, rows), side * LANES : (side + 1) * LANES].astype(jnp.float32) for f in range(4)
                ]
                raws.append(raw)
                some, clean = classify(raw, marks, pairs)
                color.append(some)
                clear.append(clean)
            for f in range(4):
                for g in range(2):
                    part = slice(SUB * g, SUB * g + SUB)
                    both = jnp.where(wide < 64, raws[0][f][part], raws[1][f][part])
                    begin = 64 * g + 8 * k
                    both = pltpu.roll(both, (begin + 3) % LANES, 1)
                    pltpu.store(packed_ref.at[f, spot], both, mask=(wide >= begin) & (wide < begin + 8))
            alpha = [1.0 - c for c in clear]
            if through is None:
                add(0, alpha, color)
                through = clear
                continue
            near = [t * (1.0 - frac) for t in through] if frac else through
            add(whole, [w * a for w, a in zip(turned(near, -whole), alpha)], color)
            after = [n * c for n, c in zip(near, turned(clear, whole))]
            if frac:
                far = [t * frac for t in through]
                add(whole + 1, [w * a for w, a in zip(turned(far, -whole - 1), alpha)], color)
                after = [p + n * c for p, n, c in zip(after, far, turned(clear, whole + 1))]
            through = after
        reach = plan[-1][0] + 2
        done = []
        for c in range(3):
            moved = [turned(sums[s, c], s) for s in range(reach)]
            done.append([sum(m[side] for m in moved) for side in range(2)])
        done.append([CODE * CODE - CODE * CODE * t for t in through])
        lane = lax.broadcasted_iota(jnp.int32, (TILE, LANES), 1)
        for r in range(rows // TILE):
            tile = (rows // TILE) * j + r
            row = lax.broadcasted_iota(jnp.int32, (TILE, LANES), 0) + (first + tile * TILE)
            live = [(row >= live_ref[0]) & (row < live_ref[1])]
            live.append(live[0] | (lane >= own_columns))
            for side in range(2):
                codes = [encode(done[c][side][r * TILE : (r + 1) * TILE], live[side]) for c in range(4)]
                out_ref[tile, :, side * LANES : (side + 1) * LANES] = jnp.concatenate(codes, axis=0).astype(jnp.int16)
        return carry

    lax.fori_loop(0, BLOCK // rows, group, 0, unroll=UNROLL)
    rim_ref[...] = packed_ref[...].astype(rim_ref.dtype)


def brick(breakpoints, tf_color, tf_opacity, live, fields):
    _, slices, height, width = fields.shape
    smem = pl.BlockSpec(memory_space=pltpu.SMEM)
    return pl.pallas_call(
        functools.partial(brick_kernel, slices),
        grid=(height // BLOCK,),
        in_specs=[smem, smem, smem, smem, pl.BlockSpec((4, slices, BLOCK, width), lambda i: (0, 0, i, 0))],
        out_specs=[
            pl.BlockSpec((BLOCK // TILE, 4 * TILE, width), lambda i: (i, 0, 0)),
            pl.BlockSpec((4, HALF, LANES), lambda i: (0, i, 0)),
        ],
        out_shape=[
            jax.ShapeDtypeStruct((height // TILE, 4 * TILE, width), jnp.int16),
            jax.ShapeDtypeStruct((4, height // 2, LANES), jnp.bfloat16),
        ],
        scratch_shapes=[pltpu.VMEM((4, HALF, LANES), jnp.float32)],
        compiler_params=pltpu.CompilerParams(vmem_limit_bytes=40 * 1024 * 1024),
        cost_estimate=pl.CostEstimate(flops=60 * slices * height * width, bytes_accessed=8 * slices * height * width, transcendentals=0),
        name="brick",
    )(breakpoints, tf_color, tf_opacity, live, fields)


def image_kernel(count_x, count_z, order_ref, codes_ref, out_ref):
    lane = lax.broadcasted_iota(jnp.int32, (4 * TILE, LANES), 1)

    def column(i, carry):
        def layer(k, state):
            image, through = list(state[:2]), list(state[2:])
            d = order_ref[i, k]
            moved = 3 * d
            own = i * count_z + d
            behind = jnp.maximum(i - 1, 0) * count_z + d
            left = codes_ref[own, :, :LANES].astype(jnp.int32)
            right = codes_ref[own, :, LANES:].astype(jnp.int32)
            before = codes_ref[behind, :, LANES:].astype(jnp.int32)
            before = jnp.where((left[:, :1] < 0) | (i == 0), 0, before)
            tail = lane >= LANES - moved
            for side, piece in enumerate((jnp.where(tail, before, left), jnp.where(tail, left, right))):
                root = jnp.maximum(pltpu.roll(piece, moved, 1), 0).astype(jnp.float32) * (1.0 / CODE)
                piece = root * root
                t = through[side]
                image[side] = image[side] + jnp.concatenate([t, t, t], axis=0) * piece[: 3 * TILE]
                through[side] = t - t * piece[3 * TILE :]
            return (*image, *through)

        none = jnp.zeros((3 * TILE, LANES), jnp.float32)
        clear = jnp.ones((TILE, LANES), jnp.float32)
        state = lax.fori_loop(0, count_z, layer, (none, none, clear, clear), unroll=DEPTHS)
        image, through = state[:2], state[2:]
        for side in range(2):
            at = pl.multiple_of((2 * i + side) * LANES, LANES)
            for c in range(3):
                out_ref[c, :, pl.ds(at, LANES)] = image[side][c * TILE : (c + 1) * TILE]
            out_ref[3, :, pl.ds(at, LANES)] = 1.0 - through[side]
        return carry

    lax.fori_loop(0, count_x, column, 0, unroll=COLUMNS)


def compose(order, codes, count_x, count_z):
    vmem = pl.BlockSpec(memory_space=pltpu.VMEM)
    return pl.pallas_call(
        functools.partial(image_kernel, count_x, count_z),
        in_specs=[pl.BlockSpec(memory_space=pltpu.SMEM), vmem],
        out_specs=vmem,
        out_shape=jax.ShapeDtypeStruct((4, TILE, count_x * 2 * LANES), jnp.float32),
        compiler_params=pltpu.CompilerParams(vmem_limit_bytes=40 * 1024 * 1024),
        name="compose",
    )(order, codes)


def per_device(fields, breakpoints, tf_color, tf_opacity, depth_order, live_rows):
    count_x, count_z = lax.axis_size("bx"), lax.axis_size("bz")
    live = live_rows.reshape(2)
    tf = (breakpoints, tf_color, tf_opacity, live)
    codes, rim = brick(*tf, fields)
    behind = lax.ppermute(rim, "bx", [(i, i + 1) for i in range(count_x - 1)])
    codes = with_edges(fields.shape[1], *tf, behind, rim, codes)
    codes = lax.all_to_all(codes, ("bx", "bz"), split_axis=0, concat_axis=0, tiled=True)
    return compose(depth_order, codes, count_x, count_z)


def solution(mesh):
    return jax.shard_map(
        per_device,
        mesh=mesh,
        in_specs=(P(None, "bz", None, "bx"), P(), P(), P(), P(), P("bx", "bz", None)),
        out_specs=P(None, ("bx", "bz"), None),
        check_vma=False,
    )
```

time: 99.3 us -> 99.2 us (level)
  waiting for transfers between devices: 32.7 us -> 41 us
  Pallas kernels: 45 us -> 37.3 us
  starting transfers between devices: 19.1 us -> 16.5 us
  local copies, waits for them, and re-layouts: 2.14 us -> 4.13 us
    ppermute x1, waiting for transfers between devices: 0.01 us -> 10.5 us  [per_device(): behind = lax.ppermute(rim, 'bx', [(i, i + 1) for i in range(count_x - 1)])]
    pallas_call x2 -> x1, Pallas kernels: 14.6 us -> 4.59 us  [with_edges(): pl.pallas_call(functools.partial(edge_kernel, slices), in_specs=[smem, sm...]
    unnamed x12 -> x16, local copies, waits for them, and re-layouts: 0.17 us -> 4.13 us
    ppermute x1 -> x0, waiting for transfers between devices: 2.25 us -> none  [per_device(): lax.ppermute(live, 'bx', [(i + 1, i) for i in range(count_x - 1)])]
    pallas_call x1, Pallas kernels: 26.1 us -> 27.9 us  [brick(): pl.pallas_call(functools.partial(brick_kernel, slices), grid=(height // B...]
    another operation x1 -> x0, local copies, waits for them, and re-layouts: 1.33 us -> none  [per_device(): jnp.stack([(here > 0).astype(jnp.int32), live[0], live[1], next_live[0],...]
    ppermute x1 -> x0, starting transfers between devices: 1.29 us -> none  [per_device(): lax.ppermute(live, 'bx', [(i + 1, i) for i in range(count_x - 1)])]
    all_to_all x1, starting transfers between devices: 13.8 us -> 12.5 us  [per_device(): lax.all_to_all(codes, ('bx', 'bz'), split_axis=0, concat_axis=0, tiled=True)]
  transfers between devices with their start and end apart: 3 -> 2, of which waited for: 2 -> 2; matrix products, arithmetic and copies ran while one was open for 2% -> 0% of each run, Pallas kernels for 26% -> 0%
where the time goes in v3:
time: 99.2 us; the launch traced here: 98.9 us
  waiting for transfers between devices  41 us (41%)
  Pallas kernels  37.3 us (38%)
  starting transfers between devices  16.5 us (17%)
  local copies, waits for them, and re-layouts  4.13 us (4%)
    all_to_all x1, waiting for transfers between devices, per_device(): lax.all_to_all(codes, ('bx', 'bz'), split_axis=0, concat_axis=0, tiled=True)  30.4 us
    pallas_call x1, Pallas kernels, brick(): pl.pallas_call(functools.partial(brick_kernel, slices), grid=(height // B...  27.9 us
    all_to_all x1, starting transfers between devices, per_device(): lax.all_to_all(codes, ('bx', 'bz'), split_axis=0, concat_axis=0, tiled=True)  12.5 us
    ppermute x1, waiting for transfers between devices, per_device(): behind = lax.ppermute(rim, 'bx', [(i, i + 1) for i in range(count_x - 1)])  10.5 us
    pallas_call x1, Pallas kernels, compose(): pl.pallas_call(functools.partial(image_kernel, count_x, count_z), in_spec...  4.73 us
    pallas_call x1, Pallas kernels, with_edges(): pl.pallas_call(functools.partial(edge_kernel, slices), in_specs=[smem, sm...  4.59 us
    unnamed x16, local copies, waits for them, and re-layouts  4.13 us
    ppermute x1, starting transfers between devices, per_device(): behind = lax.ppermute(rim, 'bx', [(i, i + 1) for i in range(count_x - 1)])  3.98 us
  transfers between devices with their start and end apart: 2, of which 2 were waited for; matrix products, arithmetic and copies ran while one was open for 0% of the time, Pallas kernels for 0%

profile of v3, /device:TPU:1, one launch (start us, length us, event | category | flops | bytes accessed | tf_op | source)
XLA Modules:
  0.0 98.9 jit_solution(17552175368309642616)
XLA Ops:
  0.0 0.8 copy.8.color_ref
  0.8 0.0 copy-start.1
  0.8 0.7 copy-done.1
  1.4 0.0 copy-start.3
  1.4 0.7 copy-done.3
  2.1 0.0 copy-start.5
  2.1 0.7 copy-done.5
  2.7 0.0 copy-start.2
  2.7 0.0 copy-start.4
  2.7 27.9 %brick.1 = (s16[128,32,256]{2,1,0:T(8,128)(2,1)S(1)}, bf16[4,512,128]{2,1,0:T(8,128)(2,1)S(1)}) custom-call(s32[8]{0:T(128)S(1)} %copy-done.1, f32[8,3]{1,0:T(8,128)S(1)} %copy.8.color_ref, f32[8]{0:T(128)S(1)} %copy-done.3, s32[2]{0:T(128)S(1)} %bitcast.1, bf16[4,8,1024,256]{3,2,1,0:T(8,128)(2,1)} %fields_ref.1), custom_call_target="tpu_custom_call" | custom-call | flops 125829120 | bytes 16777216 | tf_op jit(solution)/shard_map/brick/pallas_call | solution.py:242
  30.7 4.0 %collective-permute-start = (bf16[4,512,128]{2,1,0:T(8,128)(2,1)S(1)}, bf16[4,512,128]{2,1,0:T(8,128)(2,1)S(1)}, u32[]{:S(2)}, u32[]{:S(2)}) collective-permute-start(bf16[4,512,128]{2,1,0:T(8,128)(2,1)S(1)} %get-tuple-element.7.own_ref), channel_id=1, source_target_pairs={{0,8},{8,16},{16,24},{24,32},{32,40},{40,48},{48,56},{56,64},{64,7... | collective-permute-start | bytes 1572872 | tf_op jit(solution)/shard_map/ppermute | solution.py:315
  34.7 10.5 %collective-permute-done.halo_ref = bf16[4,512,128]{2,1,0:T(8,128)(2,1)S(1)} collective-permute-done((bf16[4,512,128]{2,1,0:T(8,128)(2,1)S(1)}, bf16[4,512,128]{2,1,0:T(8,128)(2,1)S(1)}, u32[]{:S(2)}, u32[]{:S(2)}) %collective-permute-start) | collective-permute-done | bytes 524320 | tf_op jit(solution)/shard_map/ppermute | solution.py:315
  45.2 0.0 copy-done.2
  45.2 0.0 copy-done.4
  45.2 4.6 %edges.1 = s16[128,32,256]{2,1,0:T(8,128)(2,1)S(1)} custom-call(s32[8]{0:T(128)S(1)} %copy-done.2, f32[8,3]{1,0:T(8,128)S(1)} %copy.8.color_ref, f32[8]{0:T(128)S(1)} %copy-done.4, s32[2]{0:T(128)S(1)} %bitcast.2, bf16[4,512,128]{2,1,0:T(8,128)(2,1)S(1)} %collective-permute-done.halo_ref, bf16[4,512,128]{2,1,0:T(8,128)(2,1)S(1)} %get-tuple-element.7.own_ref, ...), custom_call_target="tpu_custom_call" | custom-call | tf_op jit(solution)/shard_map/edges/pallas_call | solution.py:157
  49.8 0.0 copy-start
  49.8 1.3 %copy-done = s16[128,32,256]{2,1,0:T(8,128)(2,1)} copy-done((s16[128,32,256]{2,1,0:T(8,128)(2,1)}, s16[128,32,256]{2,1,0:T(8,128)(2,1)S(1)}, u32[]{:S(2)}) %copy-start) | copy-done | bytes 2097176
  51.1 0.0 copy-start.6
  51.1 12.5 %all-to-all-start = ((s16[128,32,256]{2,1,0:T(8,128)(2,1)}), s16[128,32,256]{2,1,0:T(8,128)(2,1)S(1)}, u32[]{:S(2)}, u32[]{:S(2)}) async-start(s16[128,32,256]{2,1,0:T(8,128)(2,1)} %copy-done), calls=%async_computation | async-start | bytes 4194304 | tf_op jit(solution)/shard_map/all_to_all | solution.py:317
  63.7 0.0 copy-done.6
  63.7 0.1 copy.9.order_ref
  63.8 30.4 %all-to-all-done.codes_ref = s16[128,32,256]{2,1,0:T(8,128)(2,1)S(1)} async-done(((s16[128,32,256]{2,1,0:T(8,128)(2,1)}), s16[128,32,256]{2,1,0:T(8,128)(2,1)S(1)}, u32[]{:S(2)}, u32[]{:S(2)}) %all-to-all-start) | async-done | bytes 2097184 | tf_op jit(solution)/shard_map/all_to_all | solution.py:317
  94.2 4.7 %compose.1 = f32[4,8,4096]{2,1,0:T(8,128)} custom-call(s32[16,8]{1,0:T(8,128)S(1)} %copy.9.order_ref, s16[128,32,256]{2,1,0:T(8,128)(2,1)S(1)} %all-to-all-done.codes_ref), custom_call_target="tpu_custom_call" | custom-call | tf_op jit(solution)/shard_map/compose/pallas_call | solution.py:300
Async XLA Ops:
  0.8 0.7 copy-start.1
  1.4 0.7 copy-start.3
  2.1 0.7 copy-start.5
  2.7 42.5 %copy-start.2 = (s32[8]{0:T(128)S(1)}, s32[8]{0:T(128)}, u32[]{:S(2)}) copy-start(s32[8]{0:T(128)} %bp_ref.3) | copy-start | bytes 100
  2.7 42.5 %copy-start.4 = (f32[8]{0:T(128)S(1)}, f32[8]{0:T(128)}, u32[]{:S(2)}) copy-start(f32[8]{0:T(128)} %opacity_ref.3) | copy-start | bytes 100
  30.7 14.5 %collective-permute-start = (bf16[4,512,128]{2,1,0:T(8,128)(2,1)S(1)}, bf16[4,512,128]{2,1,0:T(8,128)(2,1)S(1)}, u32[]{:S(2)}, u32[]{:S(2)}) collective-permute-start(bf16[4,512,128]{2,1,0:T(8,128)(2,1)S(1)} %get-tuple-element.7.own_ref), channel_id=1, source_target_pairs={{0,8},{8,16},{16,24},{24,32},{32,40},{40,48},{48,56},{56,64},{64,7... | collective-permute-start | bytes 1572872 | tf_op jit(solution)/shard_map/ppermute | solution.py:315
  49.8 1.3 %copy-start = (s16[128,32,256]{2,1,0:T(8,128)(2,1)}, s16[128,32,256]{2,1,0:T(8,128)(2,1)S(1)}, u32[]{:S(2)}) copy-start(s16[128,32,256]{2,1,0:T(8,128)(2,1)S(1)} %edges.1) | copy-start | bytes 6291460
  51.1 12.5 %copy-start.6 = (s32[16,8]{0,1:T(8,128)S(1)}, s32[16,8]{0,1:T(8,128)}, u32[]{:S(2)}) copy-start(s32[16,8]{0,1:T(8,128)} %param.10) | copy-start | bytes 1540
  51.1 43.1 %all-to-all-start = ((s16[128,32,256]{2,1,0:T(8,128)(2,1)}), s16[128,32,256]{2,1,0:T(8,128)(2,1)S(1)}, u32[]{:S(2)}, u32[]{:S(2)}) async-start(s16[128,32,256]{2,1,0:T(8,128)(2,1)} %copy-done), calls=%async_computation | async-start | bytes 4194304 | tf_op jit(solution)/shard_map/all_to_all | solution.py:317

commit v4 on v3

--- a/solution.py
+++ b/solution.py
@@ -18,6 +18,8 @@
 EDGES = 512
 COLUMNS = 1
 PATCH = 4
+RIMS = 256
+COPIES = 8
 DEPTHS = 8
 CODE = 32767.0
 LOG2E = 1.4426950408889634
@@ -121,7 +123,7 @@
     return result + [CODE * CODE - CODE * CODE * product]
 
 
-def edge_kernel(slices, bp_ref, color_ref, opacity_ref, live_ref, halo_ref, own_ref, codes_ref, out_ref, edge_ref):
+def edge_kernel(slices, bp_ref, color_ref, opacity_ref, live_ref, halo_ref, own_ref, codes_ref, out_ref, edge_ref, full_ref, sems):
     marks, pairs = tables(bp_ref, color_ref, opacity_ref)
     has_left = lax.axis_index("bx")
     lane = lax.broadcasted_iota(jnp.int32, (EDGES, LANES), 1)
@@ -144,11 +146,24 @@
                 at = pl.ds(pl.multiple_of((j * count + t) * TILE, TILE), TILE)
                 edge = jnp.concatenate([edge_ref[c, at, :] for c in range(4)], axis=0)
                 codes = jnp.where(lane < 3, pltpu.roll(edge, turn, 1), codes_ref[tile, :, :LANES].astype(jnp.int32))
-                out_ref[tile, :, :LANES] = codes.astype(jnp.int16)
-                out_ref[tile, :, LANES:] = codes_ref[tile, :, LANES:]
-        return carry
-
-    lax.fori_loop(0, codes_ref.shape[0] // (2 * count), patch, 0, unroll=PATCH)
+                full_ref[tile, :, :LANES] = codes.astype(jnp.int16)
+                full_ref[tile, :, LANES:] = codes_ref[tile, :, LANES:]
+        return carry
+
+    steps_each = codes_ref.shape[0] // (2 * count) // COPIES
+
+    def move(part):
+        tiles = pl.ds(part * (codes_ref.shape[0] // COPIES), codes_ref.shape[0] // COPIES)
+        return pltpu.make_async_copy(full_ref.at[tiles], out_ref.at[tiles], sems.at[part])
+
+    def leave(part, carry):
+        lax.fori_loop(0, steps_each, lambda j, c: patch(part * steps_each + j, c), 0, unroll=PATCH)
+        move(part).start()
+        return carry
+
+    lax.fori_loop(0, COPIES, leave, 0)
+    for part in range(COPIES):
+        move(part).wait()
 
 
 def with_edges(slices, breakpoints, tf_color, tf_opacity, live, halo, own, codes):
@@ -157,25 +172,27 @@
     return pl.pallas_call(
         functools.partial(edge_kernel, slices),
         in_specs=[smem, smem, smem, smem, vmem, vmem, vmem],
-        out_specs=vmem,
-        out_shape=jax.ShapeDtypeStruct(codes.shape, codes.dtype),
-        scratch_shapes=[pltpu.VMEM((4, halo.shape[1], LANES), jnp.int32)],
+        out_specs=pl.BlockSpec(memory_space=pltpu.HBM),
+        out_shape=pltpu.HBM(codes.shape, codes.dtype),
+        scratch_shapes=[
+            pltpu.VMEM((4, halo.shape[1], LANES), jnp.int32),
+            pltpu.VMEM(codes.shape, codes.dtype),
+            pltpu.SemaphoreType.DMA((COPIES,)),
+        ],
         compiler_params=pltpu.CompilerParams(vmem_limit_bytes=40 * 1024 * 1024),
         name="edges",
     )(breakpoints, tf_color, tf_opacity, live, halo, own, codes)
 
 
-def brick_kernel(slices, bp_ref, color_ref, opacity_ref, live_ref, fields_ref, out_ref, rim_ref, packed_ref):
+def brick_kernel(slices, bp_ref, color_ref, opacity_ref, live_ref, fields_ref, out_ref):
     marks, pairs = tables(bp_ref, color_ref, opacity_ref)
     plan = steps(slices)
     first = pl.program_id(0) * BLOCK
     rows = GROUP
-    wide = lax.broadcasted_iota(jnp.int32, (SUB, LANES), 1)
     own_columns = LANES - 3 * lax.axis_index("bz")
 
     def group(j, carry):
         base = pl.multiple_of(j * rows, rows)
-        spot = pl.ds(pl.multiple_of(j * SUB, SUB), SUB)
         sums = {}
 
         def add(s, weight, color):
@@ -186,22 +203,14 @@
         through = None
         for k in range(slices):
             whole, frac = plan[k]
-            color, clear, raws = [], [], []
+            color, clear = [], []
             for side in range(2):
                 raw = [
                     fields_ref[f, k, pl.ds(base, rows), side * LANES : (side + 1) * LANES].astype(jnp.float32) for f in range(4)
                 ]
-                raws.append(raw)
                 some, clean = classify(raw, marks, pairs)
                 color.append(some)
                 clear.append(clean)
-            for f in range(4):
-                for g in range(2):
-                    part = slice(SUB * g, SUB * g + SUB)
-                    both = jnp.where(wide < 64, raws[0][f][part], raws[1][f][part])
-                    begin = 64 * g + 8 * k
-                    both = pltpu.roll(both, (begin + 3) % LANES, 1)
-                    pltpu.store(packed_ref.at[f, spot], both, mask=(wide >= begin) & (wide < begin + 8))
             alpha = [1.0 - c for c in clear]
             if through is None:
                 add(0, alpha, color)
@@ -233,7 +242,6 @@
         return carry
 
     lax.fori_loop(0, BLOCK // rows, group, 0, unroll=UNROLL)
-    rim_ref[...] = packed_ref[...].astype(rim_ref.dtype)
 
 
 def brick(breakpoints, tf_color, tf_opacity, live, fields):
@@ -243,19 +251,49 @@
         functools.partial(brick_kernel, slices),
         grid=(height // BLOCK,),
         in_specs=[smem, smem, smem, smem, pl.BlockSpec((4, slices, BLOCK, width), lambda i: (0, 0, i, 0))],
-        out_specs=[
-            pl.BlockSpec((BLOCK // TILE, 4 * TILE, width), lambda i: (i, 0, 0)),
-            pl.BlockSpec((4, HALF, LANES), lambda i: (0, i, 0)),
-        ],
-        out_shape=[
-            jax.ShapeDtypeStruct((height // TILE, 4 * TILE, width), jnp.int16),
-            jax.ShapeDtypeStruct((4, height // 2, LANES), jnp.bfloat16),
-        ],
-        scratch_shapes=[pltpu.VMEM((4, HALF, LANES), jnp.float32)],
+        out_specs=pl.BlockSpec((BLOCK // TILE, 4 * TILE, width), lambda i: (i, 0, 0)),
+        out_shape=jax.ShapeDtypeStruct((height // TILE, 4 * TILE, width), jnp.int16),
         compiler_params=pltpu.CompilerParams(vmem_limit_bytes=40 * 1024 * 1024),
         cost_estimate=pl.CostEstimate(flops=60 * slices * height * width, bytes_accessed=8 * slices * height * width, transcendentals=0),
         name="brick",
     )(breakpoints, tf_color, tf_opacity, live, fields)
+
+
+def rim_kernel(slices, fields_ref, rim_ref):
+    rows = 4 * SUB
+    lane = lax.broadcasted_iota(jnp.int32, (2 * SUB, LANES), 1)
+
+    def group(j, carry):
+        base = pl.multiple_of(j * rows, rows)
+        for f in range(4):
+            total = jnp.zeros((2 * SUB, LANES), jnp.float32)
+            for k in range(slices):
+                left = fields_ref[f, k, pl.ds(base, rows), :LANES].astype(jnp.float32)
+                right = fields_ref[f, k, pl.ds(base, rows), LANES:].astype(jnp.float32)
+                parts = [slice(SUB * p, SUB * (p + 1)) for p in range(4)]
+                for g in range(2):
+                    both = [jnp.where(lane[:SUB] < 64, left[p], right[p]) for p in parts[g::2]]
+                    begin = 64 * g + 8 * k
+                    both = pltpu.roll(jnp.concatenate(both, axis=0), (begin + 3) % LANES, 1)
+                    total = jnp.where((lane >= begin) & (lane < begin + 8), both, total)
+            rim_ref[f, pl.ds(pl.multiple_of(j * 2 * SUB, 2 * SUB), 2 * SUB), :] = total.astype(rim_ref.dtype)
+        return carry
+
+    lax.fori_loop(0, RIMS // rows, group, 0, unroll=2)
+
+
+def rims(fields):
+    _, slices, height, width = fields.shape
+    return pl.pallas_call(
+        functools.partial(rim_kernel, slices),
+        grid=(height // RIMS,),
+        in_specs=[pl.BlockSpec((4, slices, RIMS, width), lambda i: (0, 0, i, 0))],
+        out_specs=pl.BlockSpec((4, RIMS // 2, LANES), lambda i: (0, i, 0)),
+        out_shape=jax.ShapeDtypeStruct((4, height // 2, LANES), jnp.bfloat16),
+        compiler_params=pltpu.CompilerParams(vmem_limit_bytes=40 * 1024 * 1024),
+        cost_estimate=pl.CostEstimate(flops=4 * slices * height * width, bytes_accessed=8 * slices * height * width, transcendentals=0),
+        name="rims",
+    )(fields)
 
 
 def image_kernel(count_x, count_z, order_ref, codes_ref, out_ref):
@@ -271,9 +309,9 @@
             left = codes_ref[own, :, :LANES].astype(jnp.int32)
             right = codes_ref[own, :, LANES:].astype(jnp.int32)
             before = codes_ref[behind, :, LANES:].astype(jnp.int32)
-            before = jnp.where((left[:, :1] < 0) | (i == 0), 0, before)
+            before = jnp.where(i == 0, 0, before)
             tail = lane >= LANES - moved
-            for side, piece in enumerate((jnp.where(tail, before, left), jnp.where(tail, left, right))):
+            for side, piece in enumerate((jnp.where(tail & (left >= 0), before, left), jnp.where(tail, left, right))):
                 root = jnp.maximum(pltpu.roll(piece, moved, 1), 0).astype(jnp.float32) * (1.0 / CODE)
                 piece = root * root
                 t = through[side]
@@ -311,9 +349,9 @@
     count_x, count_z = lax.axis_size("bx"), lax.axis_size("bz")
     live = live_rows.reshape(2)
     tf = (breakpoints, tf_color, tf_opacity, live)
-    codes, rim = brick(*tf, fields)
+    rim = rims(fields)
     behind = lax.ppermute(rim, "bx", [(i, i + 1) for i in range(count_x - 1)])
-    codes = with_edges(fields.shape[1], *tf, behind, rim, codes)
+    codes = with_edges(fields.shape[1], *tf, behind, rim, brick(*tf, fields))
     codes = lax.all_to_all(codes, ("bx", "bz"), split_axis=0, concat_axis=0, tiled=True)
     return compose(depth_order, codes, count_x, count_z)
 

time: 99.2 us -> 87.4 us (0.88)
  waiting for transfers between devices: 41 us -> 30.4 us
  Pallas kernels: 37.3 us -> 41.9 us
  local copies, waits for them, and re-layouts: 4.13 us -> 0.18 us
  starting transfers between devices: 16.5 us -> 14.6 us
    ppermute x1, waiting for transfers between devices: 10.5 us -> 0.01 us  [per_device(): behind = lax.ppermute(rim, 'bx', [(i, i + 1) for i in range(count_x - 1)])]
    pallas_call x0 -> x1, Pallas kernels: none -> 7.86 us  [rims(): pl.pallas_call(functools.partial(rim_kernel, slices), grid=(height // RIM...]
    unnamed x16 -> x12, local copies, waits for them, and re-layouts: 4.13 us -> 0.18 us
    pallas_call x1, Pallas kernels: 27.9 us -> 24.9 us  [brick(): pl.pallas_call(functools.partial(brick_kernel, slices), grid=(height // B...]
    all_to_all x1, starting transfers between devices: 12.5 us -> 10.6 us  [per_device(): lax.all_to_all(codes, ('bx', 'bz'), split_axis=0, concat_axis=0, tiled=True)]
  transfers between devices with their start and end apart: 2 -> 2, of which waited for: 2 -> 1; matrix products, arithmetic and copies ran while one was open for 0% -> 0% of each run, Pallas kernels for 0% -> 29%
where the time goes in v4:
time: 87.4 us; the launch traced here: 87.2 us
  Pallas kernels  41.9 us (48%)
  waiting for transfers between devices  30.4 us (35%)
  starting transfers between devices  14.6 us (17%)
    all_to_all x1, waiting for transfers between devices, per_device(): lax.all_to_all(codes, ('bx', 'bz'), split_axis=0, concat_axis=0, tiled=True)  30.4 us
    pallas_call x1, Pallas kernels, brick(): pl.pallas_call(functools.partial(brick_kernel, slices), grid=(height // B...  24.9 us
    all_to_all x1, starting transfers between devices, per_device(): lax.all_to_all(codes, ('bx', 'bz'), split_axis=0, concat_axis=0, tiled=True)  10.6 us
    pallas_call x1, Pallas kernels, rims(): pl.pallas_call(functools.partial(rim_kernel, slices), grid=(height // RIM...  7.86 us
    pallas_call x1, Pallas kernels, with_edges(): pl.pallas_call(functools.partial(edge_kernel, slices), in_specs=[smem, sm...  5.37 us
    ppermute x1, starting transfers between devices, per_device(): behind = lax.ppermute(rim, 'bx', [(i, i + 1) for i in range(count_x - 1)])  3.98 us
    pallas_call x1, Pallas kernels, compose(): pl.pallas_call(functools.partial(image_kernel, count_x, count_z), in_spec...  3.75 us
  transfers between devices with their start and end apart: 2, of which 1 were waited for; matrix products, arithmetic and copies ran while one was open for 0% of the time, Pallas kernels for 29%

profile of v4, /device:TPU:1, one launch (start us, length us, event | category | flops | bytes accessed | tf_op | source)
XLA Modules:
  0.0 87.2 jit_solution(505975287876110320)
XLA Ops:
  0.0 0.0 copy-start.4
  0.0 0.0 copy-start.2
  0.0 0.0 copy-start
  0.0 0.0 copy-start.1
  0.0 7.9 %rims.1.own_ref = bf16[4,512,128]{2,1,0:T(8,128)(2,1)S(1)} custom-call(bf16[4,8,1024,256]{3,2,1,0:T(8,128)(2,1)} %fields_ref.3), custom_call_target="tpu_custom_call" | custom-call | flops 8388608 | bytes 16777216 | tf_op jit(solution)/shard_map/rims/pallas_call | solution.py:287
  7.9 4.0 %collective-permute-start = (bf16[4,512,128]{2,1,0:T(8,128)(2,1)S(1)}, bf16[4,512,128]{2,1,0:T(8,128)(2,1)S(1)}, u32[]{:S(2)}, u32[]{:S(2)}) collective-permute-start(bf16[4,512,128]{2,1,0:T(8,128)(2,1)S(1)} %rims.1.own_ref), channel_id=1, source_target_pairs={{0,8},{8,16},{16,24},{24,32},{32,40},{40,48},{48,56},{56,64},{64,7... | collective-permute-start | bytes 1572872 | tf_op jit(solution)/shard_map/ppermute | solution.py:353
  11.9 0.0 copy-done.4
  11.9 0.1 copy.8.color_ref
  12.0 0.0 copy-done.2
  12.0 0.0 copy-done
  12.0 0.0 copy-done.1
  12.0 24.9 %brick.1.codes_ref = s16[128,32,256]{2,1,0:T(8,128)(2,1)S(1)} custom-call(s32[8]{0:T(128)S(1)} %copy-done, f32[8,3]{1,0:T(8,128)S(1)} %copy.8.color_ref, f32[8]{0:T(128)S(1)} %copy-done.1, s32[2]{0:T(128)S(1)} %bitcast.1, bf16[4,8,1024,256]{3,2,1,0:T(8,128)(2,1)} %fields_ref.3), custom_call_target="tpu_custom_call" | custom-call | flops 125829120 | bytes 16777216 | tf_op jit(solution)/shard_map/brick/pallas_call | solution.py:250
  36.9 0.0 collective-permute-done.halo_ref
  36.9 5.4 %edges.1 = s16[128,32,256]{2,1,0:T(8,128)(2,1)} custom-call(s32[8]{0:T(128)S(1)} %copy-done, f32[8,3]{1,0:T(8,128)S(1)} %copy.8.color_ref, f32[8]{0:T(128)S(1)} %copy-done.1, s32[2]{0:T(128)S(1)} %bitcast.2, bf16[4,512,128]{2,1,0:T(8,128)(2,1)S(1)} %collective-permute-done.halo_ref, bf16[4,512,128]{2,1,0:T(8,128)(2,1)S(1)} %rims.1.own_ref, ...), custom_call_target="tpu_custom_call" | custom-call | tf_op jit(solution)/shard_map/edges/pallas_call | solution.py:172
  42.2 0.0 copy-start.3
  42.3 10.6 %all-to-all-start = ((s16[128,32,256]{2,1,0:T(8,128)(2,1)}), s16[128,32,256]{2,1,0:T(8,128)(2,1)S(1)}, u32[]{:S(2)}, u32[]{:S(2)}) async-start(s16[128,32,256]{2,1,0:T(8,128)(2,1)} %edges.1), calls=%async_computation | async-start | bytes 4194304 | tf_op jit(solution)/shard_map/all_to_all | solution.py:355
  52.9 0.0 copy-done.3
  52.9 0.1 copy.9.order_ref
  53.0 30.4 %all-to-all-done.codes_ref = s16[128,32,256]{2,1,0:T(8,128)(2,1)S(1)} async-done(((s16[128,32,256]{2,1,0:T(8,128)(2,1)}), s16[128,32,256]{2,1,0:T(8,128)(2,1)S(1)}, u32[]{:S(2)}, u32[]{:S(2)}) %all-to-all-start) | async-done | bytes 2097184 | tf_op jit(solution)/shard_map/all_to_all | solution.py:355
  83.4 3.8 %compose.1 = f32[4,8,4096]{2,1,0:T(8,128)} custom-call(s32[16,8]{1,0:T(8,128)S(1)} %copy.9.order_ref, s16[128,32,256]{2,1,0:T(8,128)(2,1)S(1)} %all-to-all-done.codes_ref), custom_call_target="tpu_custom_call" | custom-call | tf_op jit(solution)/shard_map/compose/pallas_call | solution.py:338
Async XLA Ops:
  0.0 11.9 %copy-start.4 = (f32[8,3]{0,1:T(4,128)S(1)}, f32[8,3]{0,1:T(4,128)}, u32[]{:S(2)}) copy-start(f32[8,3]{0,1:T(4,128)} %param.8) | copy-start | bytes 292
  0.0 12.0 %copy-start.2 = (s32[1,1,2]{2,1,0:T(1,128)S(1)}, s32[1,1,2]{2,1,0:T(1,128)}, u32[]{:S(2)}) copy-start(s32[1,1,2]{2,1,0:T(1,128)} %param.11) | copy-start | bytes 28
  0.0 12.0 %copy-start = (s32[8]{0:T(128)S(1)}, s32[8]{0:T(128)}, u32[]{:S(2)}) copy-start(s32[8]{0:T(128)} %bp_ref.3) | copy-start | bytes 100
  0.0 12.0 %copy-start.1 = (f32[8]{0:T(128)S(1)}, f32[8]{0:T(128)}, u32[]{:S(2)}) copy-start(f32[8]{0:T(128)} %opacity_ref.3) | copy-start | bytes 100
  7.9 29.0 %collective-permute-start = (bf16[4,512,128]{2,1,0:T(8,128)(2,1)S(1)}, bf16[4,512,128]{2,1,0:T(8,128)(2,1)S(1)}, u32[]{:S(2)}, u32[]{:S(2)}) collective-permute-start(bf16[4,512,128]{2,1,0:T(8,128)(2,1)S(1)} %rims.1.own_ref), channel_id=1, source_target_pairs={{0,8},{8,16},{16,24},{24,32},{32,40},{40,48},{48,56},{56,64},{64,7... | collective-permute-start | bytes 1572872 | tf_op jit(solution)/shard_map/ppermute | solution.py:353
  42.2 10.7 %copy-start.3 = (s32[16,8]{0,1:T(8,128)S(1)}, s32[16,8]{0,1:T(8,128)}, u32[]{:S(2)}) copy-start(s32[16,8]{0,1:T(8,128)} %param.10) | copy-start | bytes 1540
  42.3 41.2 %all-to-all-start = ((s16[128,32,256]{2,1,0:T(8,128)(2,1)}), s16[128,32,256]{2,1,0:T(8,128)(2,1)S(1)}, u32[]{:S(2)}, u32[]{:S(2)}) async-start(s16[128,32,256]{2,1,0:T(8,128)(2,1)} %edges.1), calls=%async_computation | async-start | bytes 4194304 | tf_op jit(solution)/shard_map/all_to_all | solution.py:355

commit v5 on v4

--- a/solution.py
+++ b/solution.py
@@ -16,10 +16,10 @@
 SUB = GROUP // 2
 UNROLL = 2
 EDGES = 512
-COLUMNS = 1
-PATCH = 4
+COLUMNS = 2
+PATCH = 8
 RIMS = 256
-COPIES = 8
+COPIES = 4
 DEPTHS = 8
 CODE = 32767.0
 LOG2E = 1.4426950408889634
@@ -134,18 +134,19 @@
         live = (line + 2 * EDGES * part >= live_ref[0]) & (line + 2 * EDGES * part < live_ref[1])
         halo, own = halo_ref[:, rows, :], own_ref[:, rows, :]
         for c, value in enumerate(boundary(halo, own, has_left, marks, pairs, slices)):
-            edge_ref[c, rows, :] = encode(value, live)
+            codes = encode(value, live)
+            for g in range(2):
+                edge_ref[g, c, rows, :] = pltpu.roll(codes, (2 * LANES - (64 * g + 8 * (slices - 1) + 3)) % LANES, 1)
     lane = lax.broadcasted_iota(jnp.int32, (4 * TILE, LANES), 1)
     count = SUB // TILE
 
     def patch(j, carry):
         for g in range(2):
-            turn = (2 * LANES - (64 * g + 8 * (slices - 1) + 3)) % LANES
             for t in range(count):
                 tile = (2 * j + g) * count + t
                 at = pl.ds(pl.multiple_of((j * count + t) * TILE, TILE), TILE)
-                edge = jnp.concatenate([edge_ref[c, at, :] for c in range(4)], axis=0)
-                codes = jnp.where(lane < 3, pltpu.roll(edge, turn, 1), codes_ref[tile, :, :LANES].astype(jnp.int32))
+                edge = jnp.concatenate([edge_ref[g, c, at, :] for c in range(4)], axis=0)
+                codes = jnp.where(lane < 3, edge, codes_ref[tile, :, :LANES].astype(jnp.int32))
                 full_ref[tile, :, :LANES] = codes.astype(jnp.int16)
                 full_ref[tile, :, LANES:] = codes_ref[tile, :, LANES:]
         return carry
@@ -175,7 +176,7 @@
         out_specs=pl.BlockSpec(memory_space=pltpu.HBM),
         out_shape=pltpu.HBM(codes.shape, codes.dtype),
         scratch_shapes=[
-            pltpu.VMEM((4, halo.shape[1], LANES), jnp.int32),
+            pltpu.VMEM((2, 4, halo.shape[1], LANES), jnp.int32),
             pltpu.VMEM(codes.shape, codes.dtype),
             pltpu.SemaphoreType.DMA((COPIES,)),
         ],

time: 87.4 us -> 86.3 us (0.987)
  Pallas kernels: 41.9 us -> 40.8 us
where the time goes in v5:
time: 86.3 us; the launch traced here: 86.1 us
  Pallas kernels  40.8 us (47%)
  waiting for transfers between devices  30.4 us (35%)
  starting transfers between devices  14.6 us (17%)
    all_to_all x1, waiting for transfers between devices, per_device(): lax.all_to_all(codes, ('bx', 'bz'), split_axis=0, concat_axis=0, tiled=True)  30.4 us
    pallas_call x1, Pallas kernels, brick(): pl.pallas_call(functools.partial(brick_kernel, slices), grid=(height // B...  24.9 us
    all_to_all x1, starting transfers between devices, per_device(): lax.all_to_all(codes, ('bx', 'bz'), split_axis=0, concat_axis=0, tiled=True)  10.6 us
    pallas_call x1, Pallas kernels, rims(): pl.pallas_call(functools.partial(rim_kernel, slices), grid=(height // RIM...  7.86 us
    pallas_call x1, Pallas kernels, with_edges(): pl.pallas_call(functools.partial(edge_kernel, slices), in_specs=[smem, sm...  4.86 us
    ppermute x1, starting transfers between devices, per_device(): behind = lax.ppermute(rim, 'bx', [(i, i + 1) for i in range(count_x - 1)])  3.98 us
    pallas_call x1, Pallas kernels, compose(): pl.pallas_call(functools.partial(image_kernel, count_x, count_z), in_spec...  3.19 us
  transfers between devices with their start and end apart: 2, of which 1 were waited for; matrix products, arithmetic and copies ran while one was open for 0% of the time, Pallas kernels for 29%

profile of v5, /device:TPU:1, one launch (start us, length us, event | category | flops | bytes accessed | tf_op | source)
XLA Modules:
  0.0 86.1 jit_solution(3874200243640275931)
XLA Ops:
  0.0 0.0 copy-start.4
  0.0 0.0 copy-start.2
  0.0 0.0 copy-start
  0.0 0.0 copy-start.1
  0.0 7.9 %rims.1.own_ref = bf16[4,512,128]{2,1,0:T(8,128)(2,1)S(1)} custom-call(bf16[4,8,1024,256]{3,2,1,0:T(8,128)(2,1)} %fields_ref.3), custom_call_target="tpu_custom_call" | custom-call | flops 8388608 | bytes 16777216 | tf_op jit(solution)/shard_map/rims/pallas_call | solution.py:288
  7.9 4.0 %collective-permute-start = (bf16[4,512,128]{2,1,0:T(8,128)(2,1)S(1)}, bf16[4,512,128]{2,1,0:T(8,128)(2,1)S(1)}, u32[]{:S(2)}, u32[]{:S(2)}) collective-permute-start(bf16[4,512,128]{2,1,0:T(8,128)(2,1)S(1)} %rims.1.own_ref), channel_id=1, source_target_pairs={{0,8},{8,16},{16,24},{24,32},{32,40},{40,48},{48,56},{56,64},{64,7... | collective-permute-start | bytes 1572872 | tf_op jit(solution)/shard_map/ppermute | solution.py:354
  11.9 0.0 copy-done.4
  11.9 0.1 copy.8.color_ref
  12.0 0.0 copy-done.2
  12.0 0.0 copy-done
  12.0 0.0 copy-done.1
  12.0 24.9 %brick.1.codes_ref = s16[128,32,256]{2,1,0:T(8,128)(2,1)S(1)} custom-call(s32[8]{0:T(128)S(1)} %copy-done, f32[8,3]{1,0:T(8,128)S(1)} %copy.8.color_ref, f32[8]{0:T(128)S(1)} %copy-done.1, s32[2]{0:T(128)S(1)} %bitcast.1, bf16[4,8,1024,256]{3,2,1,0:T(8,128)(2,1)} %fields_ref.3), custom_call_target="tpu_custom_call" | custom-call | flops 125829120 | bytes 16777216 | tf_op jit(solution)/shard_map/brick/pallas_call | solution.py:251
  36.9 0.0 collective-permute-done.halo_ref
  36.9 4.9 %edges.1 = s16[128,32,256]{2,1,0:T(8,128)(2,1)} custom-call(s32[8]{0:T(128)S(1)} %copy-done, f32[8,3]{1,0:T(8,128)S(1)} %copy.8.color_ref, f32[8]{0:T(128)S(1)} %copy-done.1, s32[2]{0:T(128)S(1)} %bitcast.2, bf16[4,512,128]{2,1,0:T(8,128)(2,1)S(1)} %collective-permute-done.halo_ref, bf16[4,512,128]{2,1,0:T(8,128)(2,1)S(1)} %rims.1.own_ref, ...), custom_call_target="tpu_custom_call" | custom-call | tf_op jit(solution)/shard_map/edges/pallas_call | solution.py:173
  41.7 0.0 copy-start.3
  41.7 10.6 %all-to-all-start = ((s16[128,32,256]{2,1,0:T(8,128)(2,1)}), s16[128,32,256]{2,1,0:T(8,128)(2,1)S(1)}, u32[]{:S(2)}, u32[]{:S(2)}) async-start(s16[128,32,256]{2,1,0:T(8,128)(2,1)} %edges.1), calls=%async_computation | async-start | bytes 4194304 | tf_op jit(solution)/shard_map/all_to_all | solution.py:356
  52.4 0.0 copy-done.3
  52.4 0.1 copy.9.order_ref
  52.5 30.4 %all-to-all-done.codes_ref = s16[128,32,256]{2,1,0:T(8,128)(2,1)S(1)} async-done(((s16[128,32,256]{2,1,0:T(8,128)(2,1)}), s16[128,32,256]{2,1,0:T(8,128)(2,1)S(1)}, u32[]{:S(2)}, u32[]{:S(2)}) %all-to-all-start) | async-done | bytes 2097184 | tf_op jit(solution)/shard_map/all_to_all | solution.py:356
  82.9 3.2 %compose.1 = f32[4,8,4096]{2,1,0:T(8,128)} custom-call(s32[16,8]{1,0:T(8,128)S(1)} %copy.9.order_ref, s16[128,32,256]{2,1,0:T(8,128)(2,1)S(1)} %all-to-all-done.codes_ref), custom_call_target="tpu_custom_call" | custom-call | tf_op jit(solution)/shard_map/compose/pallas_call | solution.py:339
Async XLA Ops:
  0.0 11.9 %copy-start.4 = (f32[8,3]{0,1:T(4,128)S(1)}, f32[8,3]{0,1:T(4,128)}, u32[]{:S(2)}) copy-start(f32[8,3]{0,1:T(4,128)} %param.8) | copy-start | bytes 292
  0.0 12.0 %copy-start.2 = (s32[1,1,2]{2,1,0:T(1,128)S(1)}, s32[1,1,2]{2,1,0:T(1,128)}, u32[]{:S(2)}) copy-start(s32[1,1,2]{2,1,0:T(1,128)} %param.11) | copy-start | bytes 28
  0.0 12.0 %copy-start = (s32[8]{0:T(128)S(1)}, s32[8]{0:T(128)}, u32[]{:S(2)}) copy-start(s32[8]{0:T(128)} %bp_ref.3) | copy-start | bytes 100
  0.0 12.0 %copy-start.1 = (f32[8]{0:T(128)S(1)}, f32[8]{0:T(128)}, u32[]{:S(2)}) copy-start(f32[8]{0:T(128)} %opacity_ref.3) | copy-start | bytes 100
  7.9 29.0 %collective-permute-start = (bf16[4,512,128]{2,1,0:T(8,128)(2,1)S(1)}, bf16[4,512,128]{2,1,0:T(8,128)(2,1)S(1)}, u32[]{:S(2)}, u32[]{:S(2)}) collective-permute-start(bf16[4,512,128]{2,1,0:T(8,128)(2,1)S(1)} %rims.1.own_ref), channel_id=1, source_target_pairs={{0,8},{8,16},{16,24},{24,32},{32,40},{40,48},{48,56},{56,64},{64,7... | collective-permute-start | bytes 1572872 | tf_op jit(solution)/shard_map/ppermute | solution.py:354
  41.7 10.7 %copy-start.3 = (s32[16,8]{0,1:T(8,128)S(1)}, s32[16,8]{0,1:T(8,128)}, u32[]{:S(2)}) copy-start(s32[16,8]{0,1:T(8,128)} %param.10) | copy-start | bytes 1540
  41.7 41.2 %all-to-all-start = ((s16[128,32,256]{2,1,0:T(8,128)(2,1)}), s16[128,32,256]{2,1,0:T(8,128)(2,1)S(1)}, u32[]{:S(2)}, u32[]{:S(2)}) async-start(s16[128,32,256]{2,1,0:T(8,128)(2,1)} %edges.1), calls=%async_computation | async-start | bytes 4194304 | tf_op jit(solution)/shard_map/all_to_all | solution.py:356

commit v6 on v5

--- a/solution.py
+++ b/solution.py
@@ -49,7 +49,7 @@
         if c == 3:
             slope, offset = -LOG2E * slope, -LOG2E * offset
         pairs.append((offset, slope))
-    return marks, (by_segment(marks[1 : NBP - 1] + [2.0]), pairs)
+    return marks, pairs
 
 
 def looked_up(table, index):
@@ -60,13 +60,11 @@
     h = jnp.tanh(raw[0] * 0.5)
     swirl = raw[1] * raw[1] + raw[2] * raw[2] + (raw[3] * raw[3] + 0.25)
     index = jnp.zeros(h.shape, jnp.int32)
-    for j in range(2, NBP - 1, 2):
+    for j in range(1, NBP - 1):
         index = jnp.where(h >= marks[j], j, index)
-    between, pairs = pairs
     parts = []
     for r in range(0, h.shape[0], TILE):
         segment, level = index[r : r + TILE], h[r : r + TILE]
-        segment = jnp.where(level >= looked_up(between, segment), segment + 1, segment)
         parts.append([looked_up(offset, segment) + looked_up(slope, segment) * level for offset, slope in pairs])
     looked = [p[0] if len(p) == 1 else jnp.concatenate(p, axis=0) for p in zip(*parts)]
     return looked[:3], jnp.exp2(looked[3] * swirl)

time: 86.3 us -> 85.7 us (level)
  transfers between devices with their start and end apart: 2 -> 2, of which waited for: 1 -> 1; matrix products, arithmetic and copies ran while one was open for 0% -> 0% of each run, Pallas kernels for 29% -> 28%
where the time goes in v6:
time: 85.7 us; the launch traced here: 85.5 us
  Pallas kernels  40.2 us (47%)
  waiting for transfers between devices  30.4 us (35%)
  starting transfers between devices  14.6 us (17%)
    all_to_all x1, waiting for transfers between devices, per_device(): lax.all_to_all(codes, ('bx', 'bz'), split_axis=0, concat_axis=0, tiled=True)  30.4 us
    pallas_call x1, Pallas kernels, brick(): pl.pallas_call(functools.partial(brick_kernel, slices), grid=(height // B...  24.3 us
    all_to_all x1, starting transfers between devices, per_device(): lax.all_to_all(codes, ('bx', 'bz'), split_axis=0, concat_axis=0, tiled=True)  10.6 us
    pallas_call x1, Pallas kernels, rims(): pl.pallas_call(functools.partial(rim_kernel, slices), grid=(height // RIM...  7.86 us
    pallas_call x1, Pallas kernels, with_edges(): pl.pallas_call(functools.partial(edge_kernel, slices), in_specs=[smem, sm...  4.83 us
    ppermute x1, starting transfers between devices, per_device(): behind = lax.ppermute(rim, 'bx', [(i, i + 1) for i in range(count_x - 1)])  3.98 us
    pallas_call x1, Pallas kernels, compose(): pl.pallas_call(functools.partial(image_kernel, count_x, count_z), in_spec...  3.19 us
  transfers between devices with their start and end apart: 2, of which 1 were waited for; matrix products, arithmetic and copies ran while one was open for 0% of the time, Pallas kernels for 28%

profile of v6, /device:TPU:1, one launch (start us, length us, event | category | flops | bytes accessed | tf_op | source)
XLA Modules:
  0.0 85.5 jit_solution(13157406862739341715)
XLA Ops:
  0.0 0.0 copy-start.4
  0.0 0.0 copy-start.2
  0.0 0.0 copy-start
  0.0 0.0 copy-start.1
  0.0 7.9 %rims.1.own_ref = bf16[4,512,128]{2,1,0:T(8,128)(2,1)S(1)} custom-call(bf16[4,8,1024,256]{3,2,1,0:T(8,128)(2,1)} %fields_ref.3), custom_call_target="tpu_custom_call" | custom-call | flops 8388608 | bytes 16777216 | tf_op jit(solution)/shard_map/rims/pallas_call | solution.py:286
  7.9 4.0 %collective-permute-start = (bf16[4,512,128]{2,1,0:T(8,128)(2,1)S(1)}, bf16[4,512,128]{2,1,0:T(8,128)(2,1)S(1)}, u32[]{:S(2)}, u32[]{:S(2)}) collective-permute-start(bf16[4,512,128]{2,1,0:T(8,128)(2,1)S(1)} %rims.1.own_ref), channel_id=1, source_target_pairs={{0,8},{8,16},{16,24},{24,32},{32,40},{40,48},{48,56},{56,64},{64,7... | collective-permute-start | bytes 1572872 | tf_op jit(solution)/shard_map/ppermute | solution.py:352
  11.9 0.0 copy-done.4
  11.9 0.1 copy.8.color_ref
  12.0 0.0 copy-done.2
  12.0 0.0 copy-done
  12.0 0.0 copy-done.1
  12.0 24.3 %brick.1.codes_ref = s16[128,32,256]{2,1,0:T(8,128)(2,1)S(1)} custom-call(s32[8]{0:T(128)S(1)} %copy-done, f32[8,3]{1,0:T(8,128)S(1)} %copy.8.color_ref, f32[8]{0:T(128)S(1)} %copy-done.1, s32[2]{0:T(128)S(1)} %bitcast.1, bf16[4,8,1024,256]{3,2,1,0:T(8,128)(2,1)} %fields_ref.3), custom_call_target="tpu_custom_call" | custom-call | flops 125829120 | bytes 16777216 | tf_op jit(solution)/shard_map/brick/pallas_call | solution.py:249
  36.3 0.0 collective-permute-done.halo_ref
  36.3 4.8 %edges.1 = s16[128,32,256]{2,1,0:T(8,128)(2,1)} custom-call(s32[8]{0:T(128)S(1)} %copy-done, f32[8,3]{1,0:T(8,128)S(1)} %copy.8.color_ref, f32[8]{0:T(128)S(1)} %copy-done.1, s32[2]{0:T(128)S(1)} %bitcast.2, bf16[4,512,128]{2,1,0:T(8,128)(2,1)S(1)} %collective-permute-done.halo_ref, bf16[4,512,128]{2,1,0:T(8,128)(2,1)S(1)} %rims.1.own_ref, ...), custom_call_target="tpu_custom_call" | custom-call | tf_op jit(solution)/shard_map/edges/pallas_call | solution.py:171
  41.1 0.0 copy-start.3
  41.1 10.6 %all-to-all-start = ((s16[128,32,256]{2,1,0:T(8,128)(2,1)}), s16[128,32,256]{2,1,0:T(8,128)(2,1)S(1)}, u32[]{:S(2)}, u32[]{:S(2)}) async-start(s16[128,32,256]{2,1,0:T(8,128)(2,1)} %edges.1), calls=%async_computation | async-start | bytes 4194304 | tf_op jit(solution)/shard_map/all_to_all | solution.py:354
  51.8 0.0 copy-done.3
  51.8 0.1 copy.9.order_ref
  51.8 30.4 %all-to-all-done.codes_ref = s16[128,32,256]{2,1,0:T(8,128)(2,1)S(1)} async-done(((s16[128,32,256]{2,1,0:T(8,128)(2,1)}), s16[128,32,256]{2,1,0:T(8,128)(2,1)S(1)}, u32[]{:S(2)}, u32[]{:S(2)}) %all-to-all-start) | async-done | bytes 2097184 | tf_op jit(solution)/shard_map/all_to_all | solution.py:354
  82.3 3.2 %compose.1 = f32[4,8,4096]{2,1,0:T(8,128)} custom-call(s32[16,8]{1,0:T(8,128)S(1)} %copy.9.order_ref, s16[128,32,256]{2,1,0:T(8,128)(2,1)S(1)} %all-to-all-done.codes_ref), custom_call_target="tpu_custom_call" | custom-call | tf_op jit(solution)/shard_map/compose/pallas_call | solution.py:337
Async XLA Ops:
  0.0 11.9 %copy-start.4 = (f32[8,3]{0,1:T(4,128)S(1)}, f32[8,3]{0,1:T(4,128)}, u32[]{:S(2)}) copy-start(f32[8,3]{0,1:T(4,128)} %param.8) | copy-start | bytes 292
  0.0 12.0 %copy-start.2 = (s32[1,1,2]{2,1,0:T(1,128)S(1)}, s32[1,1,2]{2,1,0:T(1,128)}, u32[]{:S(2)}) copy-start(s32[1,1,2]{2,1,0:T(1,128)} %param.11) | copy-start | bytes 28
  0.0 12.0 %copy-start = (s32[8]{0:T(128)S(1)}, s32[8]{0:T(128)}, u32[]{:S(2)}) copy-start(s32[8]{0:T(128)} %bp_ref.3) | copy-start | bytes 100
  0.0 12.0 %copy-start.1 = (f32[8]{0:T(128)S(1)}, f32[8]{0:T(128)}, u32[]{:S(2)}) copy-start(f32[8]{0:T(128)} %opacity_ref.3) | copy-start | bytes 100
  7.9 28.4 %collective-permute-start = (bf16[4,512,128]{2,1,0:T(8,128)(2,1)S(1)}, bf16[4,512,128]{2,1,0:T(8,128)(2,1)S(1)}, u32[]{:S(2)}, u32[]{:S(2)}) collective-permute-start(bf16[4,512,128]{2,1,0:T(8,128)(2,1)S(1)} %rims.1.own_ref), channel_id=1, source_target_pairs={{0,8},{8,16},{16,24},{24,32},{32,40},{40,48},{48,56},{56,64},{64,7... | collective-permute-start | bytes 1572872 | tf_op jit(solution)/shard_map/ppermute | solution.py:352
  41.1 10.7 %copy-start.3 = (s32[16,8]{0,1:T(8,128)S(1)}, s32[16,8]{0,1:T(8,128)}, u32[]{:S(2)}) copy-start(s32[16,8]{0,1:T(8,128)} %param.10) | copy-start | bytes 1540
  41.1 41.2 %all-to-all-start = ((s16[128,32,256]{2,1,0:T(8,128)(2,1)}), s16[128,32,256]{2,1,0:T(8,128)(2,1)S(1)}, u32[]{:S(2)}, u32[]{:S(2)}) async-start(s16[128,32,256]{2,1,0:T(8,128)(2,1)} %edges.1), calls=%async_computation | async-start | bytes 4194304 | tf_op jit(solution)/shard_map/all_to_all | solution.py:354

commit v7 on v6

--- a/solution.py
+++ b/solution.py
@@ -122,6 +122,9 @@
 
 
 def edge_kernel(slices, bp_ref, color_ref, opacity_ref, live_ref, halo_ref, own_ref, codes_ref, out_ref, edge_ref, full_ref, sems):
+    right = pl.ds(LANES, LANES)
+    whole = pltpu.make_async_copy(codes_ref.at[:, :, right], out_ref.at[:, :, right], sems.at[COPIES])
+    whole.start()
     marks, pairs = tables(bp_ref, color_ref, opacity_ref)
     has_left = lax.axis_index("bx")
     lane = lax.broadcasted_iota(jnp.int32, (EDGES, LANES), 1)
@@ -145,15 +148,14 @@
                 at = pl.ds(pl.multiple_of((j * count + t) * TILE, TILE), TILE)
                 edge = jnp.concatenate([edge_ref[g, c, at, :] for c in range(4)], axis=0)
                 codes = jnp.where(lane < 3, edge, codes_ref[tile, :, :LANES].astype(jnp.int32))
-                full_ref[tile, :, :LANES] = codes.astype(jnp.int16)
-                full_ref[tile, :, LANES:] = codes_ref[tile, :, LANES:]
+                full_ref[tile] = codes.astype(jnp.int16)
         return carry
 
     steps_each = codes_ref.shape[0] // (2 * count) // COPIES
 
     def move(part):
         tiles = pl.ds(part * (codes_ref.shape[0] // COPIES), codes_ref.shape[0] // COPIES)
-        return pltpu.make_async_copy(full_ref.at[tiles], out_ref.at[tiles], sems.at[part])
+        return pltpu.make_async_copy(full_ref.at[tiles], out_ref.at[tiles, :, pl.ds(0, LANES)], sems.at[part])
 
     def leave(part, carry):
         lax.fori_loop(0, steps_each, lambda j, c: patch(part * steps_each + j, c), 0, unroll=PATCH)
@@ -163,6 +165,7 @@
     lax.fori_loop(0, COPIES, leave, 0)
     for part in range(COPIES):
         move(part).wait()
+    whole.wait()
 
 
 def with_edges(slices, breakpoints, tf_color, tf_opacity, live, halo, own, codes):
@@ -175,8 +178,8 @@
         out_shape=pltpu.HBM(codes.shape, codes.dtype),
         scratch_shapes=[
             pltpu.VMEM((2, 4, halo.shape[1], LANES), jnp.int32),
-            pltpu.VMEM(codes.shape, codes.dtype),
-            pltpu.SemaphoreType.DMA((COPIES,)),
+            pltpu.VMEM((*codes.shape[:2], LANES), codes.dtype),
+            pltpu.SemaphoreType.DMA((COPIES + 1,)),
         ],
         compiler_params=pltpu.CompilerParams(vmem_limit_bytes=40 * 1024 * 1024),
         name="edges",
@@ -227,7 +230,7 @@
         done = []
         for c in range(3):
             moved = [turned(sums[s, c], s) for s in range(reach)]
-            done.append([sum(m[side] for m in moved) for side in range(2)])
+            done.append([functools.reduce(jnp.add, [m[side] for m in moved]) for side in range(2)])
         done.append([CODE * CODE - CODE * CODE * t for t in through])
         lane = lax.broadcasted_iota(jnp.int32, (TILE, LANES), 1)
         for r in range(rows // TILE):

time: 85.7 us -> 85.4 us (level)
  transfers between devices with their start and end apart: 2 -> 2, of which waited for: 1 -> 1; matrix products, arithmetic and copies ran while one was open for 0% -> 0% of each run, Pallas kernels for 28% -> 29%
where the time goes in v7:
time: 85.4 us; the launch traced here: 85.1 us
  Pallas kernels  39.8 us (47%)
  waiting for transfers between devices  30.4 us (36%)
  starting transfers between devices  14.6 us (17%)
    all_to_all x1, waiting for transfers between devices, per_device(): lax.all_to_all(codes, ('bx', 'bz'), split_axis=0, concat_axis=0, tiled=True)  30.4 us
    pallas_call x1, Pallas kernels, brick(): pl.pallas_call(functools.partial(brick_kernel, slices), grid=(height // B...  24.3 us
    all_to_all x1, starting transfers between devices, per_device(): lax.all_to_all(codes, ('bx', 'bz'), split_axis=0, concat_axis=0, tiled=True)  10.6 us
    pallas_call x1, Pallas kernels, rims(): pl.pallas_call(functools.partial(rim_kernel, slices), grid=(height // RIM...  7.86 us
    pallas_call x1, Pallas kernels, with_edges(): pl.pallas_call(functools.partial(edge_kernel, slices), in_specs=[smem, sm...  4.48 us
    ppermute x1, starting transfers between devices, per_device(): behind = lax.ppermute(rim, 'bx', [(i, i + 1) for i in range(count_x - 1)])  3.98 us
    pallas_call x1, Pallas kernels, compose(): pl.pallas_call(functools.partial(image_kernel, count_x, count_z), in_spec...  3.19 us
  transfers between devices with their start and end apart: 2, of which 1 were waited for; matrix products, arithmetic and copies ran while one was open for 0% of the time, Pallas kernels for 29%

profile of v7, /device:TPU:1, one launch (start us, length us, event | category | flops | bytes accessed | tf_op | source)
XLA Modules:
  0.0 85.1 jit_solution(13178361090126761815)
XLA Ops:
  0.0 0.0 copy-start.4
  0.0 0.0 copy-start.2
  0.0 0.0 copy-start
  0.0 0.0 copy-start.1
  0.0 7.9 %rims.1.own_ref = bf16[4,512,128]{2,1,0:T(8,128)(2,1)S(1)} custom-call(bf16[4,8,1024,256]{3,2,1,0:T(8,128)(2,1)} %fields_ref.3), custom_call_target="tpu_custom_call" | custom-call | flops 8388608 | bytes 16777216 | tf_op jit(solution)/shard_map/rims/pallas_call | solution.py:289
  7.9 4.0 %collective-permute-start = (bf16[4,512,128]{2,1,0:T(8,128)(2,1)S(1)}, bf16[4,512,128]{2,1,0:T(8,128)(2,1)S(1)}, u32[]{:S(2)}, u32[]{:S(2)}) collective-permute-start(bf16[4,512,128]{2,1,0:T(8,128)(2,1)S(1)} %rims.1.own_ref), channel_id=1, source_target_pairs={{0,8},{8,16},{16,24},{24,32},{32,40},{40,48},{48,56},{56,64},{64,7... | collective-permute-start | bytes 1572872 | tf_op jit(solution)/shard_map/ppermute | solution.py:355
  11.9 0.0 copy-done.4
  11.9 0.1 copy.8.color_ref
  12.0 0.0 copy-done.2
  12.0 0.0 copy-done
  12.0 0.0 copy-done.1
  12.0 24.3 %brick.1.codes_ref = s16[128,32,256]{2,1,0:T(8,128)(2,1)S(1)} custom-call(s32[8]{0:T(128)S(1)} %copy-done, f32[8,3]{1,0:T(8,128)S(1)} %copy.8.color_ref, f32[8]{0:T(128)S(1)} %copy-done.1, s32[2]{0:T(128)S(1)} %bitcast.1, bf16[4,8,1024,256]{3,2,1,0:T(8,128)(2,1)} %fields_ref.3), custom_call_target="tpu_custom_call" | custom-call | flops 125829120 | bytes 16777216 | tf_op jit(solution)/shard_map/brick/pallas_call | solution.py:252
  36.3 0.0 collective-permute-done.halo_ref
  36.3 4.5 %edges.1 = s16[128,32,256]{2,1,0:T(8,128)(2,1)} custom-call(s32[8]{0:T(128)S(1)} %copy-done, f32[8,3]{1,0:T(8,128)S(1)} %copy.8.color_ref, f32[8]{0:T(128)S(1)} %copy-done.1, s32[2]{0:T(128)S(1)} %bitcast.2, bf16[4,512,128]{2,1,0:T(8,128)(2,1)S(1)} %collective-permute-done.halo_ref, bf16[4,512,128]{2,1,0:T(8,128)(2,1)S(1)} %rims.1.own_ref, ...), custom_call_target="tpu_custom_call" | custom-call | tf_op jit(solution)/shard_map/edges/pallas_call | solution.py:174
  40.7 0.0 copy-start.3
  40.8 10.6 %all-to-all-start = ((s16[128,32,256]{2,1,0:T(8,128)(2,1)}), s16[128,32,256]{2,1,0:T(8,128)(2,1)S(1)}, u32[]{:S(2)}, u32[]{:S(2)}) async-start(s16[128,32,256]{2,1,0:T(8,128)(2,1)} %edges.1), calls=%async_computation | async-start | bytes 4194304 | tf_op jit(solution)/shard_map/all_to_all | solution.py:357
  51.4 0.0 copy-done.3
  51.4 0.1 copy.9.order_ref
  51.5 30.4 %all-to-all-done.codes_ref = s16[128,32,256]{2,1,0:T(8,128)(2,1)S(1)} async-done(((s16[128,32,256]{2,1,0:T(8,128)(2,1)}), s16[128,32,256]{2,1,0:T(8,128)(2,1)S(1)}, u32[]{:S(2)}, u32[]{:S(2)}) %all-to-all-start) | async-done | bytes 2097184 | tf_op jit(solution)/shard_map/all_to_all | solution.py:357
  81.9 3.2 %compose.1 = f32[4,8,4096]{2,1,0:T(8,128)} custom-call(s32[16,8]{1,0:T(8,128)S(1)} %copy.9.order_ref, s16[128,32,256]{2,1,0:T(8,128)(2,1)S(1)} %all-to-all-done.codes_ref), custom_call_target="tpu_custom_call" | custom-call | tf_op jit(solution)/shard_map/compose/pallas_call | solution.py:340
Async XLA Ops:
  0.0 11.9 %copy-start.4 = (f32[8,3]{0,1:T(4,128)S(1)}, f32[8,3]{0,1:T(4,128)}, u32[]{:S(2)}) copy-start(f32[8,3]{0,1:T(4,128)} %param.8) | copy-start | bytes 292
  0.0 12.0 %copy-start.2 = (s32[1,1,2]{2,1,0:T(1,128)S(1)}, s32[1,1,2]{2,1,0:T(1,128)}, u32[]{:S(2)}) copy-start(s32[1,1,2]{2,1,0:T(1,128)} %param.11) | copy-start | bytes 28
  0.0 12.0 %copy-start = (s32[8]{0:T(128)S(1)}, s32[8]{0:T(128)}, u32[]{:S(2)}) copy-start(s32[8]{0:T(128)} %bp_ref.3) | copy-start | bytes 100
  0.0 12.0 %copy-start.1 = (f32[8]{0:T(128)S(1)}, f32[8]{0:T(128)}, u32[]{:S(2)}) copy-start(f32[8]{0:T(128)} %opacity_ref.3) | copy-start | bytes 100
  7.9 28.4 %collective-permute-start = (bf16[4,512,128]{2,1,0:T(8,128)(2,1)S(1)}, bf16[4,512,128]{2,1,0:T(8,128)(2,1)S(1)}, u32[]{:S(2)}, u32[]{:S(2)}) collective-permute-start(bf16[4,512,128]{2,1,0:T(8,128)(2,1)S(1)} %rims.1.own_ref), channel_id=1, source_target_pairs={{0,8},{8,16},{16,24},{24,32},{32,40},{40,48},{48,56},{56,64},{64,7... | collective-permute-start | bytes 1572872 | tf_op jit(solution)/shard_map/ppermute | solution.py:355
  40.7 10.7 %copy-start.3 = (s32[16,8]{0,1:T(8,128)S(1)}, s32[16,8]{0,1:T(8,128)}, u32[]{:S(2)}) copy-start(s32[16,8]{0,1:T(8,128)} %param.10) | copy-start | bytes 1540
  40.8 41.2 %all-to-all-start = ((s16[128,32,256]{2,1,0:T(8,128)(2,1)}), s16[128,32,256]{2,1,0:T(8,128)(2,1)S(1)}, u32[]{:S(2)}, u32[]{:S(2)}) async-start(s16[128,32,256]{2,1,0:T(8,128)(2,1)} %edges.1), calls=%async_computation | async-start | bytes 4194304 | tf_op jit(solution)/shard_map/all_to_all | solution.py:357
